TPU v7x, 512 devices: a whole 4x4x16 slice. The times are simulated.
512 devices in a mesh: row: 16 (over z), col: 32 (over y, x, core).
Axes of the slice: x: 4, y: 4, z: 16, core: 2. Of those that a mesh axis runs over, the one named last changes fastest.
Arguments:
- positions: float32 [3, 524288], P(None, ('row', 'col')), may hold values from -5 to 5
- velocities: float32 [3, 524288], P(None, ('row', 'col')), may hold values from -3 to 3
- accels: float32 [3, 524288], P(None, ('row', 'col')), may hold values from -3 to 3
- jerks: float32 [3, 524288], P(None, ('row', 'col')), may hold values from -24 to 24
- masses: float32 [1, 524288], P(None, ('row', 'col')), may hold values from 0.25 to 4
- elapsed: float32 [1, 524288], P(None, ('row', 'col')), may hold values from 0.0625 to 0.5
- active: int32 [32768], P('row'), may hold values from 0 to 524287, as said below
- live_tiles: int32 [16], P('row'), may hold values from 1 to 16, as said below
Outputs:
- new_positions: float32 [3, 524288], P(None, ('row', 'col'))
- new_velocities: float32 [3, 524288], P(None, ('row', 'col'))
- new_accels: float32 [3, 524288], P(None, ('row', 'col'))
- new_jerks: float32 [3, 524288], P(None, ('row', 'col'))
Inputs may be any that keep to these rules, and one draw needn't show every extreme that they name: `active`: all 32768 entries are different star indices, live and not. `live_tiles`: some index of row has all its tiles live in every draw.
All inputs are finite; a program needn't handle non-finite values.
Results may differ from a plain program's by a relative error of at most 0.0001.
Values sent between devices are 32-bit elements; how exact they have to be, the bound alone decides.
A program may use at most 128 MiB of HBM per device.

v0:
```python
import jax
import jax.numpy as jnp
from jax import lax
from jax.sharding import PartitionSpec as P

TILE = 128


EPS2 = 0.01


def predict(pos, vel, acc, jerk, step):
    x_pred = pos + step * (vel + step * (0.5 * acc + step * jerk / 6.0))
    v_pred = vel + step * (acc + step * (0.5 * jerk))
    return (x_pred, v_pred)


def pair_sums(i_pos, i_vel, j_pos, j_vel, j_weight):
    dx = j_pos[:, None, :] - i_pos[:, :, None]
    dv = j_vel[:, None, :] - i_vel[:, :, None]
    r_two = jnp.sum(dx * dx, axis=0) + EPS2
    inv_two = 1.0 / r_two
    scale = j_weight * jnp.sqrt(inv_two) * inv_two
    radial = 3.0 * jnp.sum(dx * dv, axis=0) * inv_two
    accel = jnp.sum(scale * dx, axis=2)
    jerk = jnp.sum(scale * (dv - radial * dx), axis=2)
    return jnp.concatenate([accel, jerk], 0)


def correct(pos, vel, acc, jerk, step, new_acc, new_jerk):
    v_new = vel + 0.5 * step * (acc + new_acc) + step * step / 12.0 * (jerk - new_jerk)
    x_new = pos + 0.5 * step * (vel + v_new) + step * step / 12.0 * (acc - new_acc)
    return (x_new, v_new)


def sweep(i_state, j_pos, j_vel, j_weight, count):
    block = min(j_pos.shape[1], 1024)
    blocks = j_pos.shape[1] // block

    def tile_step(tile, totals):
        start = tile * TILE
        tile_state = lax.dynamic_slice_in_dim(i_state, start, TILE, 1)

        def block_step(index, part):
            offset = index * block
            jp_block = lax.dynamic_slice_in_dim(j_pos, offset, block, 1)
            jv_block = lax.dynamic_slice_in_dim(j_vel, offset, block, 1)
            jw_block = lax.dynamic_slice_in_dim(j_weight, offset, block, 1)
            return part + pair_sums(tile_state[0:3], tile_state[3:6], jp_block, jv_block, jw_block)

        part = lax.fori_loop(0, blocks, block_step, jnp.zeros((6, TILE), jnp.float32))
        return lax.dynamic_update_slice_in_dim(totals, part, start, 1)

    return lax.fori_loop(0, count, tile_step, jnp.zeros((6, i_state.shape[1]), jnp.float32))


def per_device(positions, velocities, accels, jerks, masses, elapsed, active, live_tiles):
    n_row = lax.axis_size("row")
    n_col = lax.axis_size("col")
    width = positions.shape[1]
    total_stars = width * n_row * n_col
    slots = active.shape[0]
    per_row = slots // TILE
    row_index = lax.axis_index("row")
    col_index = lax.axis_index("col")
    weight = masses / total_stars
    stored = jnp.concatenate([positions, velocities, accels, jerks, weight, elapsed], 0)
    whole = lax.all_gather(stored, "row", axis=1, tiled=True)
    j_pos, j_vel = predict(whole[0:3], whole[3:6], whole[6:9], whole[9:12], whole[13:14])
    j_weight = whole[12:13]
    all_ids, all_live = (
        lax.all_gather(active, "row", axis=0, tiled=True),
        lax.all_gather(live_tiles, "row", axis=0, tiled=True),
    )
    tile_total = all_ids.shape[0] // TILE
    tile_live = jnp.arange(tile_total) % per_row < jnp.repeat(all_live, per_row)
    slot_ids = jnp.where(jnp.repeat(tile_live, TILE), all_ids, -1)
    my_count = live_tiles[0]
    my_ids = lax.dynamic_slice_in_dim(slot_ids, row_index * slots, slots)
    owner_col = my_ids // width % n_col
    local_pos = my_ids // (width * n_col) * width + my_ids % width
    mine = (my_ids >= 0) & (owner_col == col_index)
    where_at = jnp.where(mine, local_pos, 0)
    picked = jnp.take(jnp.concatenate([j_pos, j_vel], 0), where_at, axis=1)
    i_state = lax.psum(jnp.where(mine[None, :], picked, 0.0), "col")
    forces = sweep(i_state, j_pos, j_vel, j_weight, my_count)
    summed = lax.psum(forces, "col")
    delivered = lax.all_gather(summed, "row", axis=1, tiled=True)
    base = (row_index * n_col + col_index) * width
    local = slot_ids - base
    keep = (slot_ids >= 0) & (local >= 0) & (local < width)
    target = jnp.where(keep, local, width)
    new_both = jnp.zeros((6, width), jnp.float32).at[:, target].set(delivered, mode="drop")
    flag = (
        jnp.zeros((1, width), jnp.float32)
        .at[:, target]
        .set(jnp.ones((1, target.shape[0]), jnp.float32), mode="drop")
    )
    is_on = flag > 0.5
    new_acc = new_both[0:3]
    new_jerk = new_both[3:6]
    x_new, v_new = correct(positions, velocities, accels, jerks, elapsed, new_acc, new_jerk)
    return (
        jnp.where(is_on, x_new, positions),
        jnp.where(is_on, v_new, velocities),
        jnp.where(is_on, new_acc, accels),
        jnp.where(is_on, new_jerk, jerks),
    )


def solution(mesh):
    in_specs = (
        P(None, ("row", "col")),
        P(None, ("row", "col")),
        P(None, ("row", "col")),
        P(None, ("row", "col")),
        P(None, ("row", "col")),
        P(None, ("row", "col")),
        P("row"),
        P("row"),
    )
    out_specs = (
        P(None, ("row", "col")),
        P(None, ("row", "col")),
        P(None, ("row", "col")),
        P(None, ("row", "col")),
    )
    return jax.shard_map(
        per_device, mesh=mesh, in_specs=in_specs, out_specs=out_specs, check_vma=False
    )
```

profile of v0, /device:TPU:1, one launch (start us, length us, event | category | flops | bytes accessed | tf_op | source)
XLA Modules:
  0.0 979.6 jit_solution(14058858425116482398)
XLA Ops:
  0.6 1.3 dynamic-slice
  2.6 0.8 dynamic-update-slice
  3.3 23.8 %all-reduce = s32[16]{0:T(128)S(1)} all-reduce(s32[16]{0:T(128)S(1)} %dynamic-update-slice), channel_id=1, replica_groups=mesh['row'=16,'col'=32] {'row'}, use_global_device_ids=true, to_apply=%add | all-reduce | flops 16 | bytes 128
  27.3 20.9 %all_gather.13 = s32[32768]{0:T(1024)S(1)} all-gather(s32[2048]{0:T(1024)} %param.18), channel_id=1, replica_groups=mesh['row'=16,'col'=32] {'row'}, dimensions={0}, use_global_device_ids=true | all-gather | bytes 139264 | tf_op jit(solution)/shard_map/all_gather | solution.py:72
  49.1 2.3 concatenate.13
  51.4 26.3 %all_gather.14 = f32[14,16384]{1,0:T(8,128)S(1)} all-gather(f32[14,1024]{1,0:T(8,128)S(1)} %concatenate.13), channel_id=1, replica_groups=mesh['row'=16,'col'=32] {'row'}, dimensions={1}, use_global_device_ids=true | all-gather | bytes 974848 | tf_op jit(solution)/shard_map/all_gather | solution.py:68
  78.3 5.3 copy.110
  83.6 8.8 gather_fusion
  92.4 0.7 select_bitcast_fusion
  93.2 146.8 %psum.14 = f32[6,2048]{0,1:T(8,128)S(1)} all-reduce(f32[6,2048]{0,1:T(8,128)S(1)} %select_bitcast_fusion), channel_id=1, replica_groups=mesh['row'=16,'col'=32] {'col'}, use_global_device_ids=true, to_apply=%region_1.2 | all-reduce | flops 12288 | bytes 98304 | tf_op jit(solution)/shard_map/psum | solution.py:85
  240.3 332.4 %while.25 = (s32[]{:T(128)}, f32[6,2048]{1,0:T(8,128)S(1)}, s32[]{:T(128)}, f32[6,2048]{1,0:T(8,128)S(1)}, f32[1,16384]{1,0:T(1,128)S(1)}, /*index=5*/f32[3,1638...) while((s32[]{:T(128)}, f32[6,2048]{1,0:T(8,128)S(1)}, ...), condition=%wide.region_9.10_spmd, body=%wide.region_2.9_spmd.sunk | while | flops 6030861 | bytes 4344256 | solution.py:54
  241.0 23.0 %while.26 = (s32[]{:T(128)}, f32[6,128]{1,0:T(8,128)S(1)}, f32[1,16384]{1,0:T(1,128)S(1)}, f32[3,16384]{1,0:T(4,128)S(1)}, f32[6,128]{1,0:T(8,128)S(1)}, /*index...) while((s32[]{:T(128)}, f32[6,128]{1,0:T(8,128)S(1)}, ...), condition=%wide.region_8.8_spmd.clone, body=%wide.region_3.7_spmd.clone.sunk | while | flops 6030855 | bytes 4329637 | solution.py:51
  241.7 0.7 fusion.30
  246.0 0.7 fusion.30
  264.7 23.0 %while.26 = (s32[]{:T(128)}, f32[6,128]{1,0:T(8,128)S(1)}, f32[1,16384]{1,0:T(1,128)S(1)}, f32[3,16384]{1,0:T(4,128)S(1)}, f32[6,128]{1,0:T(8,128)S(1)}, /*index...) while((s32[]{:T(128)}, f32[6,128]{1,0:T(8,128)S(1)}, ...), condition=%wide.region_8.8_spmd.clone, body=%wide.region_3.7_spmd.clone.sunk | while | flops 6030855 | bytes 4329637 | solution.py:51
  288.4 23.0 %while.26 = (s32[]{:T(128)}, f32[6,128]{1,0:T(8,128)S(1)}, f32[1,16384]{1,0:T(1,128)S(1)}, f32[3,16384]{1,0:T(4,128)S(1)}, f32[6,128]{1,0:T(8,128)S(1)}, /*index...) while((s32[]{:T(128)}, f32[6,128]{1,0:T(8,128)S(1)}, ...), condition=%wide.region_8.8_spmd.clone, body=%wide.region_3.7_spmd.clone.sunk | while | flops 6030855 | bytes 4329637 | solution.py:51
  312.1 23.0 %while.26 = (s32[]{:T(128)}, f32[6,128]{1,0:T(8,128)S(1)}, f32[1,16384]{1,0:T(1,128)S(1)}, f32[3,16384]{1,0:T(4,128)S(1)}, f32[6,128]{1,0:T(8,128)S(1)}, /*index...) while((s32[]{:T(128)}, f32[6,128]{1,0:T(8,128)S(1)}, ...), condition=%wide.region_8.8_spmd.clone, body=%wide.region_3.7_spmd.clone.sunk | while | flops 6030855 | bytes 4329637 | solution.py:51
  335.8 23.0 %while.26 = (s32[]{:T(128)}, f32[6,128]{1,0:T(8,128)S(1)}, f32[1,16384]{1,0:T(1,128)S(1)}, f32[3,16384]{1,0:T(4,128)S(1)}, f32[6,128]{1,0:T(8,128)S(1)}, /*index...) while((s32[]{:T(128)}, f32[6,128]{1,0:T(8,128)S(1)}, ...), condition=%wide.region_8.8_spmd.clone, body=%wide.region_3.7_spmd.clone.sunk | while | flops 6030855 | bytes 4329637 | solution.py:51
  359.5 23.0 %while.26 = (s32[]{:T(128)}, f32[6,128]{1,0:T(8,128)S(1)}, f32[1,16384]{1,0:T(1,128)S(1)}, f32[3,16384]{1,0:T(4,128)S(1)}, f32[6,128]{1,0:T(8,128)S(1)}, /*index...) while((s32[]{:T(128)}, f32[6,128]{1,0:T(8,128)S(1)}, ...), condition=%wide.region_8.8_spmd.clone, body=%wide.region_3.7_spmd.clone.sunk | while | flops 6030855 | bytes 4329637 | solution.py:51
  383.2 23.0 %while.26 = (s32[]{:T(128)}, f32[6,128]{1,0:T(8,128)S(1)}, f32[1,16384]{1,0:T(1,128)S(1)}, f32[3,16384]{1,0:T(4,128)S(1)}, f32[6,128]{1,0:T(8,128)S(1)}, /*index...) while((s32[]{:T(128)}, f32[6,128]{1,0:T(8,128)S(1)}, ...), condition=%wide.region_8.8_spmd.clone, body=%wide.region_3.7_spmd.clone.sunk | while | flops 6030855 | bytes 4329637 | solution.py:51
  406.9 23.0 %while.26 = (s32[]{:T(128)}, f32[6,128]{1,0:T(8,128)S(1)}, f32[1,16384]{1,0:T(1,128)S(1)}, f32[3,16384]{1,0:T(4,128)S(1)}, f32[6,128]{1,0:T(8,128)S(1)}, /*index...) while((s32[]{:T(128)}, f32[6,128]{1,0:T(8,128)S(1)}, ...), condition=%wide.region_8.8_spmd.clone, body=%wide.region_3.7_spmd.clone.sunk | while | flops 6030855 | bytes 4329637 | solution.py:51
  430.5 23.0 %while.26 = (s32[]{:T(128)}, f32[6,128]{1,0:T(8,128)S(1)}, f32[1,16384]{1,0:T(1,128)S(1)}, f32[3,16384]{1,0:T(4,128)S(1)}, f32[6,128]{1,0:T(8,128)S(1)}, /*index...) while((s32[]{:T(128)}, f32[6,128]{1,0:T(8,128)S(1)}, ...), condition=%wide.region_8.8_spmd.clone, body=%wide.region_3.7_spmd.clone.sunk | while | flops 6030855 | bytes 4329637 | solution.py:51
  454.2 23.0 %while.26 = (s32[]{:T(128)}, f32[6,128]{1,0:T(8,128)S(1)}, f32[1,16384]{1,0:T(1,128)S(1)}, f32[3,16384]{1,0:T(4,128)S(1)}, f32[6,128]{1,0:T(8,128)S(1)}, /*index...) while((s32[]{:T(128)}, f32[6,128]{1,0:T(8,128)S(1)}, ...), condition=%wide.region_8.8_spmd.clone, body=%wide.region_3.7_spmd.clone.sunk | while | flops 6030855 | bytes 4329637 | solution.py:51
  477.9 23.0 %while.26 = (s32[]{:T(128)}, f32[6,128]{1,0:T(8,128)S(1)}, f32[1,16384]{1,0:T(1,128)S(1)}, f32[3,16384]{1,0:T(4,128)S(1)}, f32[6,128]{1,0:T(8,128)S(1)}, /*index...) while((s32[]{:T(128)}, f32[6,128]{1,0:T(8,128)S(1)}, ...), condition=%wide.region_8.8_spmd.clone, body=%wide.region_3.7_spmd.clone.sunk | while | flops 6030855 | bytes 4329637 | solution.py:51
  501.6 23.0 %while.26 = (s32[]{:T(128)}, f32[6,128]{1,0:T(8,128)S(1)}, f32[1,16384]{1,0:T(1,128)S(1)}, f32[3,16384]{1,0:T(4,128)S(1)}, f32[6,128]{1,0:T(8,128)S(1)}, /*index...) while((s32[]{:T(128)}, f32[6,128]{1,0:T(8,128)S(1)}, ...), condition=%wide.region_8.8_spmd.clone, body=%wide.region_3.7_spmd.clone.sunk | while | flops 6030855 | bytes 4329637 | solution.py:51
  525.3 23.0 %while.26 = (s32[]{:T(128)}, f32[6,128]{1,0:T(8,128)S(1)}, f32[1,16384]{1,0:T(1,128)S(1)}, f32[3,16384]{1,0:T(4,128)S(1)}, f32[6,128]{1,0:T(8,128)S(1)}, /*index...) while((s32[]{:T(128)}, f32[6,128]{1,0:T(8,128)S(1)}, ...), condition=%wide.region_8.8_spmd.clone, body=%wide.region_3.7_spmd.clone.sunk | while | flops 6030855 | bytes 4329637 | solution.py:51
  549.0 23.0 %while.26 = (s32[]{:T(128)}, f32[6,128]{1,0:T(8,128)S(1)}, f32[1,16384]{1,0:T(1,128)S(1)}, f32[3,16384]{1,0:T(4,128)S(1)}, f32[6,128]{1,0:T(8,128)S(1)}, /*index...) while((s32[]{:T(128)}, f32[6,128]{1,0:T(8,128)S(1)}, ...), condition=%wide.region_8.8_spmd.clone, body=%wide.region_3.7_spmd.clone.sunk | while | flops 6030855 | bytes 4329637 | solution.py:51
  572.7 123.9 %psum.15 = f32[6,2048]{1,0:T(8,128)S(1)} all-reduce(f32[6,2048]{1,0:T(8,128)S(1)} %get-tuple-element.151), channel_id=1, replica_groups=mesh['row'=16,'col'=32] {'col'}, use_global_device_ids=true, to_apply=%region_10.11 | all-reduce | flops 12288 | bytes 98304 | tf_op jit(solution)/shard_map/psum | solution.py:87
  696.6 72.1 %all_gather.15 = f32[6,32768]{1,0:T(8,128)S(1)} all-gather(f32[6,2048]{1,0:T(8,128)S(1)} %psum.15), channel_id=1, replica_groups=mesh['row'=16,'col'=32] {'row'}, dimensions={1}, use_global_device_ids=true | all-gather | bytes 835584 | tf_op jit(solution)/shard_map/all_gather | solution.py:88
  768.7 9.0 copy.112
  777.7 80.4 %scatter_custom_fusion.1 = f32[6,1024]{0,1:T(8,128)S(1)} fusion(s32[32768]{0:T(1024)S(1)} %get-tuple-element.257, f32[32768,6]{1,0:T(8,128)} %copy.112, f32[]{:T(128)} %constant.153.clone.1), kind=kCustom, calls=%fused_computation.27 | custom fusion | bytes 25088 | tf_op jit(solution)/shard_map/scatter | solution.py:93
  858.8 120.0 %scatter_custom_fusion = f32[1024]{0:T(1024)S(1)} fusion(s32[32768]{0:T(1024)S(1)} %get-tuple-element.257, f32[32768]{0:T(1024)S(1)} %broadcast.117, f32[]{:T(128)} %constant.153.clone.1), kind=kCustom, calls=%fused_computation.64 | custom fusion | bytes 4100 | tf_op jit(solution)/shard_map/scatter | solution.py:97
  (1639 shorter events, 308.2 us)
Async XLA Ops:
  858.1 120.7 %copy-start.4 = (f32[1,1024]{1,0:T(1,128)S(1)}, f32[1,1024]{1,0:T(1,128)}, u32[]{:S(2)}) copy-start(f32[1,1024]{1,0:T(1,128)} %param.17) | copy-start | bytes 12292
  858.1 120.7 %copy-start = (f32[3,1024]{1,0:T(4,128)S(1)}, f32[3,1024]{1,0:T(4,128)}, u32[]{:S(2)}) copy-start(f32[3,1024]{1,0:T(4,128)} %param.13) | copy-start | bytes 36868
  858.1 120.7 %copy-start.1 = (f32[3,1024]{1,0:T(4,128)S(1)}, f32[3,1024]{1,0:T(4,128)}, u32[]{:S(2)}) copy-start(f32[3,1024]{1,0:T(4,128)} %param.15) | copy-start | bytes 36868
  858.1 120.7 %copy-start.2 = (f32[3,1024]{1,0:T(4,128)S(1)}, f32[3,1024]{1,0:T(4,128)}, u32[]{:S(2)}) copy-start(f32[3,1024]{1,0:T(4,128)} %param.12) | copy-start | bytes 36868
  858.2 120.7 %copy-start.3 = (f32[3,1024]{1,0:T(4,128)S(1)}, f32[3,1024]{1,0:T(4,128)}, u32[]{:S(2)}) copy-start(f32[3,1024]{1,0:T(4,128)} %param.14) | copy-start | bytes 36868
where the time goes:
time: 990 us; the launch traced here: 980 us
  blocking collectives  414 us (42%)
  other arithmetic  302 us (31%)
  local copies, waits for them, and re-layouts  236 us (24%)
  loops' own time  26 us (3%)
    reduce_sum x224, other arithmetic, pair_sums(): accel = jnp.sum(scale * dx, axis=2)  160 us
    psum x1, blocking collectives, per_device(): i_state = lax.psum(jnp.where(mine[None, :], picked, 0.0), 'col')  147 us
    psum x1, blocking collectives, per_device(): summed = lax.psum(forces, 'col')  124 us
    scatter x1, local copies, waits for them, and re-layouts, per_device(): flag = jnp.zeros((1, width), jnp.float32).at[:, target].set(jnp.ones((1,...  120 us
    reduce_sum x224, other arithmetic, pair_sums(): r_two = jnp.sum(dx * dx, axis=0) + EPS2  84.5 us
    scatter x1, local copies, waits for them, and re-layouts, per_device(): jnp.zeros((6, width), jnp.float32).at[:, target].set(delivered, mode='drop')  80.4 us
    all_gather x1, blocking collectives, per_device(): delivered = lax.all_gather(summed, 'row', axis=1, tiled=True)  72.1 us
    mul x224, other arithmetic, pair_sums(): radial = 3.0 * jnp.sum(dx * dv, axis=0) * inv_two  52.8 us

commit v1 on v0

v1 whole, which is shorter than its diff:
```python
import functools

import jax
import jax.numpy as jnp
from jax import lax
from jax.experimental import pallas as pl
from jax.experimental.pallas import tpu as pltpu
from jax.sharding import PartitionSpec as P

TILE = 128
EPS2 = 0.01
LANES = 128
BLOCK_J = 2048
PIECE_J = 512
PARTS = 16
MESH = pl.DeviceIdType.MESH
VMEM = pltpu.VMEM
F32 = jnp.float32
BF16 = jnp.bfloat16


def vmem():
    return pl.BlockSpec(memory_space=pltpu.VMEM)


def smem():
    return pl.BlockSpec(memory_space=pltpu.SMEM)


def split3(x):
    high = x.astype(BF16).astype(F32)
    rest = x - high
    mid = rest.astype(BF16).astype(F32)
    return high, mid, rest - mid


class Place:
    def __init__(self, rows, cols):
        self.rows, self.cols = rows, cols
        self.side = {32: 4, 8: 2}[cols]
        self.half = self.side // 2
        self.cubes = rows // 2 * self.half * self.half
        self.row = lax.axis_index("row")
        self.col = lax.axis_index("col")
        self.y = self.col // (2 * self.side)
        self.x = lax.rem(self.col // 2, self.side)
        self.core = lax.rem(self.col, 2)
        self.cube = (self.row // 2 * self.half + self.y // 2) * self.half + self.x // 2
        self.member = self.member_at(self.row)

    def member_at(self, row):
        return ((lax.rem(row, 2) * 2 + lax.rem(self.y, 2)) * 2 + lax.rem(self.x, 2)) * 2 + self.core

    def device(self, row, y, x, core):
        return {"row": row, "col": (y * self.side + x) * 2 + core}

    def in_cube(self, member):
        return self.device(
            self.row // 2 * 2 + member // 8,
            self.y // 2 * 2 + lax.rem(member // 4, 2),
            self.x // 2 * 2 + lax.rem(member // 2, 2),
            lax.rem(member, 2),
        )

    def in_other(self, cube):
        return self.device(
            cube // (self.half * self.half) * 2 + lax.rem(self.row, 2),
            lax.rem(cube // self.half, self.half) * 2 + lax.rem(self.y, 2),
            lax.rem(cube, self.half) * 2 + lax.rem(self.x, 2),
            self.core,
        )


def signal(device):
    pl.semaphore_signal(pltpu.get_barrier_semaphore(), inc=1, device_id=device, device_id_type=MESH)


def await_greetings(count):
    pl.semaphore_wait(pltpu.get_barrier_semaphore(), count)


def each(first, last, body, step=1):
    def one(n, carry):
        body(first + n * step)
        return carry

    lax.fori_loop(0, (last - first + step - 1) // step, one, 0)


def remote(source, target, send, recv, device):
    return pltpu.make_async_remote_copy(
        src_ref=source, dst_ref=target, send_sem=send, recv_sem=recv, device_id=device, device_id_type=MESH
    )


def await_bytes(ref, semaphore):
    pltpu.make_async_copy(ref, ref, semaphore).wait()


def gather_kernel(rows, cols, total_stars, pos, vel, acc, jerk, mass, step, msg, shard, ids, id_send, id_recv, send, recv):
    at = Place(rows, cols)
    me = at.member
    each(1, PARTS, lambda d: signal(at.in_cube(lax.rem(me + d, PARTS))))
    each(1, rows, lambda d: signal({"row": lax.rem(at.row + d, rows)}))
    dt = step[...]
    a, j, v = acc[...], jerk[...], vel[...]
    shard[me, 0:3, :] = pos[...] + dt * (v + dt * (0.5 * a + dt * j / 6.0))
    shard[me, 3:4, :] = mass[...] / total_stars
    shard[me, 4:7, :] = v + dt * (a + dt * (0.5 * j))
    shard[me, 7:8, :] = jnp.ones_like(dt)
    ids[at.row] = msg[me]
    await_greetings(PARTS + rows - 2)

    def send_ids(d):
        peer = lax.rem(at.row + d, rows)
        remote(msg.at[at.member_at(peer)], ids.at[at.row], id_send, id_recv, {"row": peer}).start()

    def send_block(d):
        peer = lax.rem(me + d, PARTS)
        remote(shard.at[me], shard.at[me], send, recv, at.in_cube(peer)).start()

    each(1, rows, send_ids)
    each(1, PARTS, send_block)
    await_bytes(ids.at[pl.ds(0, rows - 1)], id_recv)
    await_bytes(ids.at[pl.ds(0, rows - 1)], id_send)
    await_bytes(shard.at[pl.ds(0, PARTS - 1)], recv)
    await_bytes(shard.at[pl.ds(0, PARTS - 1)], send)


def pick_kernel(rows, cols, width, counts, shard, ids, out, packed, table):
    at = Place(rows, cols)
    chunks = width // LANES
    high_count = PARTS * chunks
    features = (0, 1, 2, 4, 5, 6)
    groups = 4
    for order, f in enumerate(features):
        plane = jnp.concatenate([shard[:, f, c * LANES : (c + 1) * LANES] for c in range(chunks)], 0)
        h, m, l = split3(plane)
        table[order * high_count : (order + 1) * high_count, :] = jnp.concatenate([h, m, l], 1).astype(BF16)

    packed[...] = jnp.full(packed.shape, -1, jnp.int32)
    lane = lax.broadcasted_iota(jnp.int32, (8, LANES), 1)

    def pack(q, offset):
        t, shift = offset // LANES, lax.rem(offset, LANES)
        rolled = pltpu.roll(jnp.broadcast_to(ids[q, 0:1, :], (8, LANES)), shift, 1)
        packed[t] = jnp.where(lane >= shift, rolled, packed[t])
        packed[t + 1] = jnp.where(lane < shift, rolled, packed[t + 1])
        return offset + counts[q, 1, 0] * (TILE // PARTS)

    used = lax.fori_loop(0, rows, pack, 0)

    def part(g, carry):
        first = g * groups
        star = jnp.concatenate([packed[first + n, 0:1, :] for n in range(groups)], 1)
        owner = star // width
        row, col = owner // cols, lax.rem(owner, cols)
        y, x = col // (2 * at.side), lax.rem(col // 2, at.side)
        cube = (row // 2 * at.half + y // 2) * at.half + x // 2
        member = ((lax.rem(row, 2) * 2 + lax.rem(y, 2)) * 2 + lax.rem(x, 2)) * 2 + lax.rem(col, 2)
        mine = (star >= 0) & (cube == at.cube)
        place = lax.rem(star, width)
        high = jnp.where(mine, place // LANES * PARTS + member, -1)
        low = lax.rem(place, LANES)
        span = groups * LANES
        pick = jnp.where(lax.broadcasted_iota(jnp.int32, (LANES, span), 0) == low, 1.0, 0.0).astype(BF16)
        pick = jnp.concatenate([pick, pick, pick], 0)
        at_row = lax.broadcasted_iota(jnp.int32, (high_count, span), 0) == high
        for order, f in enumerate(features):
            values = jnp.dot(table[order * high_count : (order + 1) * high_count, :], pick, preferred_element_type=F32)
            found = jnp.sum(jnp.where(at_row, values, 0.0), axis=0, keepdims=True)
            for n in range(groups):
                out[2 * (first + n) + f // 4, f % 4 : f % 4 + 1, :] = found[:, n * LANES : (n + 1) * LANES]
        return carry

    out[...] = jnp.zeros_like(out)
    lax.fori_loop(0, (used + groups * LANES - 1) // (groups * LANES), part, 0)


def cube_sum_kernel(rows, cols, blocks, out, arrived, send_a, recv_a, send_b, recv_b):
    at = Place(rows, cols)
    me, cubes = at.cube, at.cubes
    share = blocks.shape[0] // cubes
    peer_of = lambda d: lax.rem(me + d, cubes)
    each(1, cubes, lambda d: signal(at.in_other(peer_of(d))))
    mine = pl.ds(me * share, share)
    arrived[me] = blocks[mine]
    await_greetings(cubes - 1)

    def scatter(d):
        peer = peer_of(d)
        remote(blocks.at[pl.ds(peer * share, share)], arrived.at[me], send_a, recv_a, at.in_other(peer)).start()

    each(1, cubes, scatter)
    await_bytes(arrived.at[pl.ds(0, cubes - 1)], recv_a)
    out[mine] = jnp.sum(arrived[...], axis=0)
    each(1, cubes, lambda d: remote(out.at[mine], out.at[mine], send_b, recv_b, at.in_other(peer_of(d))).start())
    await_bytes(out.at[pl.ds(0, (cubes - 1) * share)], recv_b)
    await_bytes(arrived.at[pl.ds(0, cubes - 1)], send_a)
    await_bytes(out.at[pl.ds(0, (cubes - 1) * share)], send_b)


def sweep_kernel(rows, cols, counts, shard, packed, states, out, j_side, j_mass):
    at = Place(rows, cols)
    width = shard.shape[2]
    total = PARTS * width
    row_of = lambda shape: lax.broadcasted_iota(jnp.int32, shape, 0)
    at8 = row_of((8, LANES))

    def dots(tile):
        first = row_of(tile.shape) < 3
        swapped = pltpu.roll(tile, 4, 0)
        norm = jnp.sum(jnp.where(first, tile * tile, 0.0), axis=0, keepdims=True)
        cross = jnp.sum(jnp.where(first, tile * swapped, 0.0), axis=0, keepdims=True)
        return norm, cross

    def prepare(z, carry):
        tile = shard[z]
        norm, cross = dots(tile)
        h, m, l = split3(tile)
        pieces = split3(norm) + split3(cross)
        line = row_of(tile.shape)
        extra = jnp.zeros_like(tile)
        for n, piece in enumerate(pieces):
            extra = jnp.where(line == n, piece, extra)
        place = pl.ds(pl.multiple_of(z * width, width), width)
        j_side[:, place] = jnp.concatenate([h, h, h, m, m, l, extra, jnp.zeros_like(tile)], 0).astype(BF16)
        h, m, l = split3(tile * tile[3:4, :])
        j_mass[:, place] = jnp.concatenate([h, m, l, jnp.zeros_like(tile)], 0).astype(BF16)
        return carry

    lax.fori_loop(0, PARTS, prepare, 0)
    out[...] = jnp.zeros_like(out)

    def left_of(tile):
        norm, cross = dots(tile)
        h, m, l = split3(tile)
        nh, nm, nl = split3(norm + EPS2)
        ch, cm, cl = split3(cross)
        zero = jnp.zeros_like(tile)

        def for_r(piece, last):
            return jnp.where(at8 < 3, -2.0 * piece, jnp.where(at8 == 7, last, 0.0))

        def for_b(piece, last):
            return jnp.where(at8 == 7, last, jnp.where(at8 == 3, 0.0, -pltpu.roll(piece, 4, 0)))

        r_extra = jnp.where(at8 < 3, 1.0, 0.0)
        b_extra = jnp.where((at8 >= 3) & (at8 < 6), 1.0, 0.0)
        blank = jnp.zeros((64, LANES), F32)
        left_r = jnp.concatenate(
            [for_r(h, nh), for_r(m, nm), for_r(l, nl), for_r(h, 0.0), for_r(m, 0.0), for_r(h, 0.0), r_extra, zero, blank], 0
        )
        left_b = jnp.concatenate(
            [for_b(h, ch), for_b(m, cm), for_b(l, cl), for_b(h, 0.0), for_b(m, 0.0), for_b(h, 0.0), b_extra, zero, blank], 0
        )
        return left_r.T[:, 0:64], left_b.T[:, 0:64]

    def run(t, count):
        span = count * LANES
        tiles = [jnp.concatenate([states[2 * (t + n)], states[2 * (t + n) + 1]], 0) for n in range(count)]
        lefts = [left_of(tile) for tile in tiles]
        left = jnp.concatenate([l[0] for l in lefts] + [l[1] for l in lefts], 0).astype(BF16)

        def one_block(n, sums):
            def place(s):
                return pl.ds(pl.multiple_of(n * BLOCK_J + s * PIECE_J, PIECE_J), PIECE_J)

            def distances(s):
                return jnp.dot(left, j_side[:, place(s)], preferred_element_type=F32)

            ahead = distances(0)
            for s in range(BLOCK_J // PIECE_J):
                both = ahead
                if s + 1 < BLOCK_J // PIECE_J:
                    ahead = distances(s + 1)
                inverse = lax.rsqrt(both[0:span])
                square = inverse * inverse
                near = square * inverse
                tilt = near * square * both[span:]
                pair = jnp.concatenate([near, tilt], 0)
                high = pair.astype(BF16)
                low = (pair - high.astype(F32)).astype(BF16)
                weights = j_mass[:, place(s)]
                sums += lax.dot_general(
                    jnp.concatenate([high, low], 1),
                    jnp.concatenate([weights, weights], 1),
                    (((1,), (1,)), ((), ())),
                    preferred_element_type=F32,
                )
            return sums

        sums = lax.fori_loop(0, total // BLOCK_J, one_block, jnp.zeros((2 * span, 32), F32))
        sums = jnp.concatenate([sums, jnp.zeros((2 * span, LANES - 32), F32)], 1)
        for n, tile in enumerate(tiles):
            near = sums[n * LANES : (n + 1) * LANES].T
            tilt = sums[span + n * LANES : span + (n + 1) * LANES].T
            near = near[0:8] + near[8:16] + near[16:24]
            tilt = tilt[0:8] + tilt[8:16] + tilt[16:24]
            near = near - tile * near[7:8]
            tilt = tilt - tile * tilt[7:8]
            force = near - jnp.where(at8 >= 4, 3.0 * pltpu.roll(tilt, 4, 0), 0.0)
            star = packed[t + n]
            force = jnp.where(star >= 0, force, 0.0)
            force = jnp.where(at8 == 3, jnp.where(at.cube == 0, star.astype(F32), 0.0), force)
            out[2 * (t + n)] = force[0:4]
            out[2 * (t + n) + 1] = force[4:8]

    live = lax.fori_loop(0, rows, lambda q, n: n + counts[q, 1, 0], 0)
    tiles = (live + PARTS - 1) // PARTS

    def two(n, carry):
        run(2 * n, 2)
        return carry

    lax.fori_loop(0, tiles // 2, two, 0)

    @pl.when(lax.rem(tiles, 2) == 1)
    def _():
        run(tiles - 1, 1)


def deliver_kernel(rows, cols, blocks, out, arrived, lined, sends, recvs):
    at = Place(rows, cols)
    me, cubes, side = at.cube, at.cubes, at.side
    share = blocks.shape[0] // cubes
    plane = side * side
    here = at.y * side + at.x
    peer_of = lambda d: lax.rem(me + d, cubes)
    sibling = at.device(at.row, at.y, at.x, 1 - at.core)

    def beside(d):
        spot = lax.rem(here + d, plane)
        return at.device(at.row, spot // side, lax.rem(spot, side), at.core)

    each(1, cubes, lambda d: signal(at.in_other(peer_of(d))))
    each(1, rows, lambda d: signal({"row": lax.rem(at.row + d, rows)}))
    each(1, plane, lambda d: signal(beside(d)))
    signal(sibling)
    arrived[me] = blocks[pl.ds(me * share, share)]
    await_greetings(cubes + rows + plane - 2)

    def scatter(d):
        peer = peer_of(d)
        part = blocks.at[pl.ds(peer * share, share)]
        remote(part, arrived.at[me], sends.at[0], recvs.at[0], at.in_other(peer)).start()

    each(1, cubes, scatter)
    others = arrived.at[pl.ds(0, cubes - 1)]
    await_bytes(others, recvs.at[0])
    lined[at.row] = jnp.sum(arrived[...], axis=0)

    def along(d):
        mine = lined.at[at.row]
        remote(mine, mine, sends.at[1], recvs.at[1], {"row": lax.rem(at.row + d, rows)}).start()

    each(1, rows, along)
    line = lined.at[pl.ds(0, rows - 1)]
    await_bytes(line, recvs.at[1])

    each(1, plane, lambda d: remote(lined, out.at[at.core, here], sends.at[2], recvs.at[2], beside(d)).start())
    remote(lined, out.at[at.core, here], sends.at[3], recvs.at[3], sibling).start()
    out[at.core, here] = lined[...]
    await_bytes(out.at[0, pl.ds(0, plane - 1)], recvs.at[2])

    def forward(d):
        block = out.at[at.core, lax.rem(here + d, plane)]
        remote(block, block, sends.at[3], recvs.at[3], sibling).start()

    each(1, plane, forward)
    await_bytes(out.at[0], recvs.at[3])
    await_bytes(others, sends.at[0])
    await_bytes(line, sends.at[1])
    await_bytes(out.at[0, pl.ds(0, plane - 1)], sends.at[2])
    await_bytes(out.at[0], sends.at[3])


def finish_kernel(
    rows, cols, counts, forces, pos, vel, acc, jerk, step, new_pos, new_vel, new_acc, new_jerk, total, lined
):
    at = Place(rows, cols)
    width = pos.shape[1]
    highs = width // LANES
    mine = at.row * cols + at.col
    features = (0, 1, 2, 4, 5, 6)
    share = forces.shape[3]
    together = 8
    at8 = lax.broadcasted_iota(jnp.int32, (highs, LANES), 0)
    at_low = lax.broadcasted_iota(jnp.int32, (LANES, LANES), 0)
    total[...] = jnp.zeros_like(total)

    def one(n, carry):
        t, first = n // (PARTS // together), lax.rem(n, PARTS // together) * together
        lefts, rights = [], []
        for k in range(together):
            member = first + k
            spots = []
            for b in range(2):
                cube = (2 * t + b) // share
                z = cube // (at.half * at.half) * 2 + member // 8
                y = lax.rem(cube // at.half, at.half) * 2 + lax.rem(member // 4, 2)
                x = lax.rem(cube, at.half) * 2 + lax.rem(member // 2, 2)
                spots.append((lax.rem(member, 2), y * at.side + x, z, lax.rem(2 * t + b, share)))
            star = forces[(*spots[0], slice(3, 4), slice(None))].astype(jnp.int32)
            ok = (star >= 0) & (star // width == mine)
            place = lax.rem(star, width)
            here = jnp.where(ok, place // LANES, -1) == at8
            low = lax.rem(place, LANES)
            rights.append(jnp.where(at_low == low, 1.0, 0.0).astype(BF16))
            pieces = [[], [], []]
            for f in features:
                row = forces[(*spots[f // 4], slice(f % 4, f % 4 + 1), slice(None))]
                for p, piece in enumerate(split3(jnp.where(here, row, 0.0))):
                    pieces[p].append(piece)
            flag = jnp.where(here, 1.0, 0.0)
            blank = jnp.zeros_like(flag)
            lefts.append(jnp.concatenate(pieces[0] + pieces[1] + pieces[2] + [flag, blank], 0).astype(BF16))
        left = jnp.concatenate(lefts, 1)
        right = jnp.concatenate(rights, 1)
        total[...] += lax.dot_general(left, right, (((1,), (1,)), ((), ())), preferred_element_type=F32)
        return carry

    live = lax.fori_loop(0, rows, lambda q, n: n + counts[q, 1, 0], 0)
    lax.fori_loop(0, (live + PARTS - 1) // PARTS * (PARTS // together), one, 0)

    for order in range(7):
        if order < 6:
            parts = [total[(p * 6 + order) * highs : (p * 6 + order + 1) * highs, :] for p in range(3)]
            plane = parts[0] + parts[1] + parts[2]
        else:
            plane = total[18 * highs : 19 * highs, :]
        for c in range(highs):
            lined[order : order + 1, c * LANES : (c + 1) * LANES] = plane[c : c + 1, :]

    on = lined[6:7, :] > 0.5
    a1, k1 = lined[0:3, :], lined[3:6, :]
    x, v, a, k, dt = pos[...], vel[...], acc[...], jerk[...], step[...]
    v1 = v + 0.5 * dt * (a + a1) + dt * dt / 12.0 * (k - k1)
    x1 = x + 0.5 * dt * (v + v1) + dt * dt / 12.0 * (a - a1)
    new_pos[...] = jnp.where(on, x1, x)
    new_vel[...] = jnp.where(on, v1, v)
    new_acc[...] = jnp.where(on, a1, a)
    new_jerk[...] = jnp.where(on, k1, k)


def params(collective_id=None, limit=48 * 2**20):
    if collective_id is None:
        return pltpu.CompilerParams(vmem_limit_bytes=limit)
    return pltpu.CompilerParams(collective_id=collective_id, has_side_effects=True, vmem_limit_bytes=limit)


def per_device(positions, velocities, accels, jerks, masses, elapsed, active, live_tiles):
    rows = lax.axis_size("row")
    cols = lax.axis_size("col")
    width = positions.shape[1]
    tiles = active.shape[0] // TILE
    unit = TILE // PARTS
    blocks = 2 * rows
    cubes = rows * cols // PARTS
    share = blocks // cubes
    plane = cols // 2
    total_stars = width * rows * cols
    dma = pltpu.SemaphoreType.DMA

    live = jnp.arange(tiles)[:, None] < live_tiles[0]
    named = jnp.where(live, active.reshape(tiles, TILE), -1)
    parts = named.reshape(tiles, PARTS, unit).transpose(1, 0, 2).reshape(PARTS, 1, LANES)
    msg = jnp.concatenate([parts, jnp.broadcast_to(live_tiles[0], parts.shape)], 1)

    shard, ids = pl.pallas_call(
        functools.partial(gather_kernel, rows, cols, total_stars),
        out_shape=(
            jax.ShapeDtypeStruct((PARTS, 8, width), F32),
            jax.ShapeDtypeStruct((rows, 2, LANES), jnp.int32),
        ),
        in_specs=[vmem()] * 7,
        out_specs=(vmem(), vmem()),
        scratch_shapes=[dma for _ in range(4)],
        compiler_params=params(0),
        name="gather_shard",
    )(positions, velocities, accels, jerks, masses, elapsed, msg)

    picked, packed = pl.pallas_call(
        functools.partial(pick_kernel, rows, cols, width),
        out_shape=(
            jax.ShapeDtypeStruct((blocks, 4, LANES), F32),
            jax.ShapeDtypeStruct((rows + 4, 8, LANES), jnp.int32),
        ),
        in_specs=[smem(), vmem(), vmem()],
        out_specs=(vmem(), vmem()),
        scratch_shapes=[VMEM((6 * PARTS * width // LANES, 3 * LANES), BF16)],
        compiler_params=params(),
        name="pick_states",
    )(ids, shard, ids)

    states = pl.pallas_call(
        functools.partial(cube_sum_kernel, rows, cols),
        out_shape=jax.ShapeDtypeStruct((blocks, 4, LANES), F32),
        in_specs=[vmem()],
        out_specs=vmem(),
        scratch_shapes=[VMEM((cubes, share, 4, LANES), F32)] + [dma for _ in range(4)],
        compiler_params=params(1),
        name="share_states",
    )(picked)

    pair_count = rows * LANES * PARTS * width
    partial = pl.pallas_call(
        functools.partial(sweep_kernel, rows, cols),
        out_shape=jax.ShapeDtypeStruct((blocks, 4, LANES), F32),
        in_specs=[smem(), vmem(), vmem(), vmem()],
        out_specs=vmem(),
        scratch_shapes=[VMEM((64, PARTS * width), BF16), VMEM((32, PARTS * width), BF16)],
        compiler_params=params(),
        cost_estimate=pl.CostEstimate(flops=200 * pair_count, bytes_accessed=2**20, transcendentals=pair_count),
        name="pair_sums",
    )(ids, shard, packed, states)

    forces = pl.pallas_call(
        functools.partial(deliver_kernel, rows, cols),
        out_shape=jax.ShapeDtypeStruct((2, plane, rows, share, 4, LANES), F32),
        in_specs=[vmem()],
        out_specs=vmem(),
        scratch_shapes=[
            VMEM((cubes, share, 4, LANES), F32),
            VMEM((rows, share, 4, LANES), F32),
            pltpu.SemaphoreType.DMA((4,)),
            pltpu.SemaphoreType.DMA((4,)),
        ],
        compiler_params=params(2),
        name="deliver_forces",
    )(partial)

    return pl.pallas_call(
        functools.partial(finish_kernel, rows, cols),
        out_shape=tuple(jax.ShapeDtypeStruct((3, width), F32) for _ in range(4)),
        in_specs=[smem()] + [vmem()] * 6,
        out_specs=(vmem(),) * 4,
        scratch_shapes=[VMEM((20 * width // LANES, LANES), F32), VMEM((8, width), F32)],
        compiler_params=params(),
        name="finish_step",
    )(ids, forces, positions, velocities, accels, jerks, elapsed)


def solution(mesh):
    stars = P(None, ("row", "col"))
    in_specs = (stars,) * 6 + (P("row"), P("row"))
    return jax.shard_map(per_device, mesh=mesh, in_specs=in_specs, out_specs=(stars,) * 4, check_vma=False)
```

time: 990 us -> 165 us (0.17)
  blocking collectives: 414 us -> 0 us
  other arithmetic: 302 us -> 0.09 us
  local copies, waits for them, and re-layouts: 236 us -> 1.67 us
  Pallas kernels: 0 us -> 161 us
  loops' own time: 26 us -> 0 us
    psum x2 -> x0, blocking collectives: 271 us -> none  [the longest x1 147 us: per_device(): i_state = lax.psum(jnp.where(mine[None, :], picked, 0.0), 'col')]
    reduce_sum x448 -> x0, other arithmetic: 244 us -> none  [the longest x224 160 us: pair_sums(): accel = jnp.sum(scale * dx, axis=2)]
    scatter x2 -> x0, local copies, waits for them, and re-layouts: 200 us -> none  [the longest x1 120 us: per_device(): flag = jnp.zeros((1, width), jnp.float32).at[:, target].set(jnp.ones((1,...]
    pallas_call x0 -> x6, Pallas kernels: none -> 161 us  [the longest x1 61.2 us: per_device(): pl.pallas_call(functools.partial(sweep_kernel, rows, cols), out_shape=jax...]
    all_gather x3 -> x0, blocking collectives: 119 us -> none  [the longest x1 72.1 us: per_device(): delivered = lax.all_gather(summed, 'row', axis=1, tiled=True)]
    mul x226 -> x0, other arithmetic: 52.8 us -> none  [the longest x224 52.8 us: pair_sums(): radial = 3.0 * jnp.sum(dx * dv, axis=0) * inv_two]
    another operation x15 -> x0, loops' own time: 26 us -> none  [the longest x14 15.5 us: tile_step(): lax.fori_loop(0, blocks, block_step, jnp.zeros((6, TILE), jnp.float32))]
    unnamed x1 -> x0, blocking collectives: 23.8 us -> none
where the time goes in v1:
time: 165 us; the launch traced here: 164 us
  Pallas kernels  161 us (98%)
  local copies, waits for them, and re-layouts  1.67 us (1%)
    pallas_call x1, Pallas kernels, per_device(): pl.pallas_call(functools.partial(sweep_kernel, rows, cols), out_shape=jax...  61.2 us
    pallas_call x1, Pallas kernels, per_device(): pl.pallas_call(functools.partial(deliver_kernel, rows, cols), out_shape=j...  39.3 us
    pallas_call x1, Pallas kernels, per_device(): pl.pallas_call(functools.partial(cube_sum_kernel, rows, cols), out_shape=...  27.2 us
    pallas_call x1, Pallas kernels, per_device(): pl.pallas_call(functools.partial(gather_kernel, rows, cols, total_stars),...  23.8 us
    pallas_call x1, Pallas kernels, per_device(): pl.pallas_call(functools.partial(finish_kernel, rows, cols), out_shape=tu...  6.34 us
    pallas_call x1, Pallas kernels, per_device(): pl.pallas_call(functools.partial(pick_kernel, rows, cols, width), out_sha...  3.37 us

profile of v1, /device:TPU:1, one launch (start us, length us, event | category | flops | bytes accessed | tf_op | source)
XLA Modules:
  0.0 164.4 jit_solution(14823001010074243956)
XLA Ops:
  1.3 0.8 reshape.26
  2.1 0.1 select_bitcast_fusion
  2.2 0.1 copy.12
  2.3 0.0 copy-start.1
  2.3 0.0 copy-start.2
  2.3 0.0 copy-start.3
  2.3 0.1 copy.13
  2.3 0.0 copy-start
  2.3 0.0 copy-start.4
  2.3 0.0 copy-start.5
  2.4 0.6 copy-done.1
  3.0 0.0 copy-done.2
  3.0 0.0 copy-done.3
  3.0 0.0 copy-done
  3.1 0.0 copy-done.4
  3.1 0.0 copy-done.5
  3.1 23.8 %gather_shard.1 = (f32[16,8,1024]{2,1,0:T(8,128)S(1)}, s32[16,2,128]{2,1,0:T(2,128)S(1)}) custom-call(f32[3,1024]{1,0:T(4,128)S(1)} %copy-done, f32[3,1024]{1,0:T(4,128)S(1)} %copy-done.1, f32[3,1024]{1,0:T(4,128)S(1)} %copy-done.2, f32[3,1024]{1,0:T(4,128)S(1)} %copy-done.3, f32[1,1024]{1,0:T(1,128)S(1)} %copy-done.5, f32[1,1024]{1,0:T(1,128)S(1)} %copy-done.4, ...), custom_call_target="tpu_custom_call" | custom-call | tf_op jit(solution)/shard_map/gather_shard/pallas_call | solution.py:470
  26.9 3.4 %pick_states.1 = (f32[32,4,128]{2,1,0:T(4,128)S(1)}, s32[20,8,128]{2,1,0:T(8,128)S(1)}) custom-call(s32[16,2,128]{2,1,0:T(2,128)S(1)} %get-tuple-element.8.counts.ids, f32[16,8,1024]{2,1,0:T(8,128)S(1)} %get-tuple-element.9.shard, s32[16,2,128]{2,1,0:T(2,128)S(1)} %get-tuple-element.8.counts.ids), custom_call_target="tpu_custom_call" | custom-call | tf_op jit(solution)/shard_map/pick_states/pallas_call | solution.py:483
  30.3 27.2 %share_states.1.states = f32[32,4,128]{2,1,0:T(4,128)S(1)} custom-call(f32[32,4,128]{2,1,0:T(4,128)S(1)} %get-tuple-element.11.blocks), custom_call_target="tpu_custom_call" | custom-call | tf_op jit(solution)/shard_map/share_states/pallas_call | solution.py:496
  57.6 61.2 %pair_sums.1.blocks = f32[32,4,128]{2,1,0:T(4,128)S(1)} custom-call(s32[16,2,128]{2,1,0:T(2,128)S(1)} %get-tuple-element.8.counts.ids, f32[16,8,1024]{2,1,0:T(8,128)S(1)} %get-tuple-element.9.shard, s32[20,8,128]{2,1,0:T(8,128)S(1)} %get-tuple-element.10.packed, f32[32,4,128]{2,1,0:T(4,128)S(1)} %share_states.1.states), custom_call_target="tpu_custom_call" | custom-call | flops 6710886400 | bytes 1048576 | tf_op jit(solution)/shard_map/pair_sums/pallas_call | solution.py:507
  118.8 39.3 %deliver_forces.1.forces = f32[2,16,16,1,4,128]{5,4,3,2,1,0:T(4,128)S(1)} custom-call(f32[32,4,128]{2,1,0:T(4,128)S(1)} %pair_sums.1.blocks), custom_call_target="tpu_custom_call" | custom-call | tf_op jit(solution)/shard_map/deliver_forces/pallas_call | solution.py:518
  158.1 6.3 %finish_step.1 = (f32[3,1024]{1,0:T(4,128)}, f32[3,1024]{1,0:T(4,128)}, f32[3,1024]{1,0:T(4,128)}, f32[3,1024]{1,0:T(4,128)}) custom-call(s32[16,2,128]{2,1,0:T(2,128)S(1)} %get-tuple-element.8.counts.ids, f32[2,16,16,1,4,128]{5,4,3,2,1,0:T(4,128)S(1)} %deliver_forces.1.forces, f32[3,1024]{1,0:T(4,128)S(1)} %copy-done, f32[3,1024]{1,0:T(4,128)S(1)} %copy-done.1, ...), custom_call_target="tpu_custom_call" | custom-call | tf_op jit(solution)/shard_map/finish_step/pallas_call | solution.py:533
  (2 shorter events, 0.0 us)
Async XLA Ops:
  2.3 0.7 copy-start.1
  2.3 0.8 copy-start.2
  2.3 0.8 copy-start.3
  2.3 0.7 copy-start
  2.3 0.7 copy-start.4
  2.3 0.7 copy-start.5

commit v2 on v1

v2 whole, which is shorter than its diff:
```python
import functools

import jax
import jax.numpy as jnp
from jax import lax
from jax.experimental import pallas as pl
from jax.experimental.pallas import tpu as pltpu
from jax.sharding import PartitionSpec as P

TILE = 128
EPS2 = 0.01
LANES = 128
BLOCK_J = 4096
PIECE_J = 1024
PARTS = 16
MESH = pl.DeviceIdType.MESH
VMEM = pltpu.VMEM
F32 = jnp.float32
BF16 = jnp.bfloat16


def vmem():
    return pl.BlockSpec(memory_space=pltpu.VMEM)


def smem():
    return pl.BlockSpec(memory_space=pltpu.SMEM)


def split3(x):
    high = x.astype(BF16).astype(F32)
    rest = x - high
    mid = rest.astype(BF16).astype(F32)
    return high, mid, rest - mid


class Place:
    def __init__(self, rows, cols):
        self.rows, self.cols = rows, cols
        self.side = {32: 4, 8: 2}[cols]
        self.half = self.side // 2
        self.quarters, self.layers = self.half * self.half, rows // 2
        self.cubes = self.quarters * self.layers
        self.row = lax.axis_index("row")
        self.col = lax.axis_index("col")
        self.y = self.col // (2 * self.side)
        self.x = lax.rem(self.col // 2, self.side)
        self.core = lax.rem(self.col, 2)
        self.quarter = self.y // 2 * self.half + self.x // 2
        self.layer = self.row // 2
        self.cube = self.quarter * self.layers + self.layer
        self.member = self.member_at(self.row)

    def member_at(self, row):
        return ((lax.rem(row, 2) * 2 + lax.rem(self.y, 2)) * 2 + lax.rem(self.x, 2)) * 2 + self.core

    def device(self, row, y, x, core):
        return {"row": row, "col": (y * self.side + x) * 2 + core}

    def in_cube(self, member):
        return self.device(
            self.layer * 2 + member // 8,
            self.y // 2 * 2 + lax.rem(member // 4, 2),
            self.x // 2 * 2 + lax.rem(member // 2, 2),
            lax.rem(member, 2),
        )

    def in_quarter(self, quarter):
        y = quarter // self.half * 2 + lax.rem(self.y, 2)
        x = lax.rem(quarter, self.half) * 2 + lax.rem(self.x, 2)
        return self.device(self.row, y, x, self.core)

    def in_layer(self, layer):
        return {"row": layer * 2 + lax.rem(self.row, 2)}


def signal(device):
    pl.semaphore_signal(pltpu.get_barrier_semaphore(), inc=1, device_id=device, device_id_type=MESH)


def await_greetings(count):
    pl.semaphore_wait(pltpu.get_barrier_semaphore(), count)


def each(first, last, body, step=1):
    def one(n, carry):
        body(first + n * step)
        return carry

    lax.fori_loop(0, (last - first + step - 1) // step, one, 0)


def remote(source, target, send, recv, device):
    return pltpu.make_async_remote_copy(
        src_ref=source, dst_ref=target, send_sem=send, recv_sem=recv, device_id=device, device_id_type=MESH
    )


def await_bytes(ref, semaphore):
    pltpu.make_async_copy(ref, ref, semaphore).wait()


def dots(tile):
    first = lax.broadcasted_iota(jnp.int32, tile.shape, 0) < 3
    swapped = pltpu.roll(tile, 4, 0)
    norm = jnp.sum(jnp.where(first, tile * tile, 0.0), axis=0, keepdims=True)
    cross = jnp.sum(jnp.where(first, tile * swapped, 0.0), axis=0, keepdims=True)
    return norm, cross


def cube_sums(at, blocks, from_quarters, from_layers, sends, recvs, meanwhile=None):
    share = blocks.shape[0] // at.cubes
    span = share * at.layers
    from_quarters[at.quarter] = blocks[pl.ds(at.quarter * span, span)]

    def to_quarter(d):
        quarter = lax.rem(at.quarter + d, at.quarters)
        part = blocks.at[pl.ds(quarter * span, span)]
        remote(part, from_quarters.at[at.quarter], sends.at[0], recvs.at[0], at.in_quarter(quarter)).start()

    rest_a = from_quarters.at[pl.ds(0, at.quarters - 1)]
    if at.quarters > 1:
        for d in range(1, at.quarters):
            to_quarter(d)
        await_bytes(rest_a, recvs.at[0])
    total = jnp.sum(from_quarters[...], axis=0)
    blocks[pl.ds(at.quarter * span, span)] = total
    from_layers[at.layer] = blocks[pl.ds(at.cube * share, share)]

    def to_layer(d):
        layer = lax.rem(at.layer + d, at.layers)
        part = blocks.at[pl.ds((at.quarter * at.layers + layer) * share, share)]
        remote(part, from_layers.at[at.layer], sends.at[1], recvs.at[1], at.in_layer(layer)).start()

    for d in range(1, at.layers):
        to_layer(d)
    if meanwhile is not None:
        meanwhile()
    rest_b = from_layers.at[pl.ds(0, at.layers - 1)]
    await_bytes(rest_b, recvs.at[1])
    left = [(rest_b, sends.at[1])]
    if at.quarters > 1:
        left.append((rest_a, sends.at[0]))
    return jnp.sum(from_layers[...], axis=0), left


def gather_kernel(
    rows,
    cols,
    total_stars,
    pos,
    vel,
    acc,
    jerk,
    mass,
    step,
    msg,
    ids,
    states,
    j_side,
    j_mass,
    shard,
    picked,
    from_quarters,
    from_layers,
    table,
    sends,
    recvs,
):
    at = Place(rows, cols)
    me, mine, cubes = at.member, at.cube, at.cubes
    share = states.shape[0] // cubes
    for d in range(1, at.quarters):
        signal(at.in_quarter(lax.rem(at.quarter + d, at.quarters)))
    each(1, rows, lambda d: signal({"row": lax.rem(at.row + d, rows)}))
    each(1, PARTS, lambda d: signal(at.in_cube(lax.rem(me + d, PARTS))))
    dt = step[...]
    a, j, v = acc[...], jerk[...], vel[...]
    shard[me, 0:3, :] = pos[...] + dt * (v + dt * (0.5 * a + dt * j / 6.0))
    shard[me, 3:4, :] = mass[...] / total_stars
    shard[me, 4:7, :] = v + dt * (a + dt * (0.5 * j))
    shard[me, 7:8, :] = jnp.ones_like(dt)
    ids[at.row] = msg[me]
    await_greetings(PARTS - 1 + rows - 1 + at.quarters - 1)

    def send_ids(d):
        peer = lax.rem(at.row + d, rows)
        remote(msg.at[at.member_at(peer)], ids.at[at.row], sends.at[4], recvs.at[4], {"row": peer}).start()

    def send_block(d):
        peer = lax.rem(me + d, PARTS)
        remote(shard.at[me], shard.at[me], sends.at[5], recvs.at[5], at.in_cube(peer)).start()

    each(1, PARTS, send_block)
    each(1, rows, send_ids)
    id_rest, shard_rest = ids.at[pl.ds(0, rows - 1)], shard.at[pl.ds(0, PARTS - 1)]
    await_bytes(shard_rest, recvs.at[5])
    await_bytes(id_rest, recvs.at[4])

    width = pos.shape[1]
    chunks = width // LANES
    high_count = PARTS * chunks
    features = (0, 1, 2, 4, 5, 6)
    groups = min(4, rows)
    for order, f in enumerate(features):
        plane = jnp.concatenate([shard[:, f, c * LANES : (c + 1) * LANES] for c in range(chunks)], 0)
        h, m, l = split3(plane)
        table[order * high_count : (order + 1) * high_count, :] = jnp.concatenate([h, m, l], 1).astype(BF16)
    picked[...] = jnp.zeros_like(picked)

    def part(g, carry):
        first = g * groups
        star = jnp.concatenate([ids[first + n, 0:1, :] for n in range(groups)], 1)
        owner = star // width
        row, col = owner // cols, lax.rem(owner, cols)
        y, x = col // (2 * at.side), lax.rem(col // 2, at.side)
        cube = (y // 2 * at.half + x // 2) * at.layers + row // 2
        member = ((lax.rem(row, 2) * 2 + lax.rem(y, 2)) * 2 + lax.rem(x, 2)) * 2 + lax.rem(col, 2)
        place = lax.rem(star, width)
        high = jnp.where((star >= 0) & (cube == mine), place // LANES * PARTS + member, -1)
        low = lax.rem(place, LANES)
        span = groups * LANES
        pick = jnp.where(lax.broadcasted_iota(jnp.int32, (LANES, span), 0) == low, 1.0, 0.0).astype(BF16)
        pick = jnp.concatenate([pick, pick, pick], 0)
        at_row = lax.broadcasted_iota(jnp.int32, (high_count, span), 0) == high
        for order, f in enumerate(features):
            values = jnp.dot(table[order * high_count : (order + 1) * high_count, :], pick, preferred_element_type=F32)
            found = jnp.sum(jnp.where(at_row, values, 0.0), axis=0, keepdims=True)
            for n in range(groups):
                picked[2 * (first + n) + f // 4, f % 4 : f % 4 + 1, :] = found[:, n * LANES : (n + 1) * LANES]
        return carry

    lax.fori_loop(0, rows // groups, part, 0)

    def prepare(z, carry):
        tile = shard[z]
        norm, cross = dots(tile)
        h, m, l = split3(tile)
        pieces = split3(norm) + split3(cross)
        line = lax.broadcasted_iota(jnp.int32, tile.shape, 0)
        extra = jnp.zeros_like(tile)
        for n, piece in enumerate(pieces):
            extra = jnp.where(line == n, piece, extra)
        blank = jnp.zeros((LANES - 56, width), F32)
        side = jnp.concatenate([h, h, h, m, m, l, extra, blank], 0)
        for c in range(chunks):
            place = pl.ds(pl.multiple_of(z * width + c * LANES, LANES), LANES)
            j_side[place, :] = side[:, c * LANES : (c + 1) * LANES].T.astype(BF16)
        h, m, l = split3(tile * tile[3:4, :])
        place = pl.ds(pl.multiple_of(z * width, width), width)
        j_mass[:, place] = jnp.concatenate([h, m, l, jnp.zeros_like(tile)], 0).astype(BF16)
        return carry

    total, left = cube_sums(
        at, picked, from_quarters, from_layers, sends, recvs, lambda: lax.fori_loop(0, PARTS // 2, prepare, 0)
    )
    own = pl.ds(mine * share, share)
    states[own] = total
    for d in range(1, at.layers):
        layer = lax.rem(at.layer + d, at.layers)
        remote(states.at[own], states.at[own], sends.at[2], recvs.at[2], at.in_layer(layer)).start()
    lax.fori_loop(PARTS // 2, PARTS, prepare, 0)
    rest = states.at[pl.ds(0, (at.layers - 1) * share)]
    await_bytes(rest, recvs.at[2])
    left.append((rest, sends.at[2]))
    span = at.layers * share
    quarter = pl.ds(at.quarter * span, span)
    if at.quarters > 1:
        for d in range(1, at.quarters):
            device = at.in_quarter(lax.rem(at.quarter + d, at.quarters))
            remote(states.at[quarter], states.at[quarter], sends.at[3], recvs.at[3], device).start()
        rest = states.at[pl.ds(0, (at.quarters - 1) * span)]
        await_bytes(rest, recvs.at[3])
        left.append((rest, sends.at[3]))
    left += [(id_rest, sends.at[4]), (shard_rest, sends.at[5])]
    for ref, semaphore in left:
        await_bytes(ref, semaphore)


def sweep_kernel(rows, cols, counts, ids, states, j_side, j_mass, out, i_tiles):
    at = Place(rows, cols)
    total = j_side.shape[0]
    at8 = lax.broadcasted_iota(jnp.int32, (8, LANES), 0)
    lane = lax.broadcasted_iota(jnp.int32, (8, LANES), 1)
    out[...] = jnp.zeros_like(out)
    i_tiles[...] = jnp.where(lax.broadcasted_iota(jnp.int32, i_tiles.shape, 1) == 3, -1.0, 0.0)

    def pack(q, offset):
        tile = jnp.concatenate([states[2 * q], states[2 * q + 1]], 0)
        tile = jnp.where(at8 == 3, ids[q, 0:1, :].astype(F32), tile)
        t, shift = offset // LANES, lax.rem(offset, LANES)
        rolled = pltpu.roll(tile, shift, 1)
        i_tiles[t] = jnp.where(lane >= shift, rolled, i_tiles[t])
        i_tiles[t + 1] = jnp.where(lane < shift, rolled, i_tiles[t + 1])
        return offset + counts[q, 1, 0] * (TILE // PARTS)

    used = lax.fori_loop(0, rows, pack, 0)

    def right_of(tile):
        norm, cross = dots(tile)
        h, m, l = split3(tile)
        nh, nm, nl = split3(norm + EPS2)
        ch, cm, cl = split3(cross)

        def for_r(piece, last):
            return jnp.where(at8 < 3, -2.0 * piece, jnp.where(at8 == 7, last, 0.0))

        def for_b(piece, last):
            return jnp.where(at8 == 7, last, jnp.where(at8 == 3, 0.0, -pltpu.roll(piece, 4, 0)))

        r_extra = jnp.where(at8 < 3, 1.0, 0.0)
        b_extra = jnp.where((at8 >= 3) & (at8 < 6), 1.0, 0.0)
        blank = jnp.zeros((LANES - 56, LANES), F32)
        right_r = jnp.concatenate(
            [for_r(h, nh), for_r(m, nm), for_r(l, nl), for_r(h, 0.0), for_r(m, 0.0), for_r(h, 0.0), r_extra, blank], 0
        )
        right_b = jnp.concatenate(
            [for_b(h, ch), for_b(m, cm), for_b(l, cl), for_b(h, 0.0), for_b(m, 0.0), for_b(h, 0.0), b_extra, blank], 0
        )
        return jnp.concatenate([right_r, right_b], 1).astype(BF16)

    def run(t, carry):
        tile = i_tiles[t]
        right = right_of(tile)

        def one_block(n, sums):
            def place(s):
                return pl.ds(pl.multiple_of(n * BLOCK_J + s * PIECE_J, PIECE_J), PIECE_J)

            def distances(s):
                return jnp.dot(j_side[place(s), :], right, preferred_element_type=F32)

            ahead = distances(0)
            for s in range(BLOCK_J // PIECE_J):
                both = ahead
                if s + 1 < BLOCK_J // PIECE_J:
                    ahead = distances(s + 1)
                inverse = lax.rsqrt(both[:, 0:LANES])
                square = inverse * inverse
                near = square * inverse
                tilt = near * square * both[:, LANES:]
                pair = jnp.concatenate([near, tilt], 1)
                high = pair.astype(BF16)
                low = (pair - high.astype(F32)).astype(BF16)
                weights = j_mass[:, place(s)]
                sums += jnp.dot(
                    jnp.concatenate([weights, weights], 1),
                    jnp.concatenate([high, low], 0),
                    preferred_element_type=F32,
                )
            return sums

        sums = lax.fori_loop(0, total // BLOCK_J, one_block, jnp.zeros((32, 2 * LANES), F32))
        sums = sums[0:8] + sums[8:16] + sums[16:24]
        near, tilt = sums[:, 0:LANES], sums[:, LANES:]
        near = near - tile * near[7:8]
        tilt = tilt - tile * tilt[7:8]
        force = near - jnp.where(at8 >= 4, 3.0 * pltpu.roll(tilt, 4, 0), 0.0)
        star = tile[3:4]
        force = jnp.where(star >= 0, force, 0.0)
        force = jnp.where(at8 == 3, jnp.where(at.cube == 0, star, 0.0), force)
        out[2 * t] = force[0:4]
        out[2 * t + 1] = force[4:8]
        return carry

    lax.fori_loop(0, (used + LANES - 1) // LANES, run, 0)


def deliver_kernel(rows, cols, partial, out, blocks, from_quarters, from_layers, lined, sends, recvs, plane_recv):
    at = Place(rows, cols)
    side = at.side
    plane = side * side
    here = at.y * side + at.x
    sibling = at.device(at.row, at.y, at.x, 1 - at.core)

    def beside(d):
        spot = lax.rem(here + d, plane)
        return at.device(at.row, spot // side, lax.rem(spot, side), at.core)

    each(1, rows, lambda d: signal({"row": lax.rem(at.row + d, rows)}))
    each(1, plane, lambda d: signal(beside(d)))
    signal(sibling)
    blocks[...] = partial[...]
    await_greetings(rows - 1 + plane)

    total, left = cube_sums(at, blocks, from_quarters, from_layers, sends, recvs)
    lined[at.row] = total
    mine = lined.at[at.row]
    for d in range(1, rows):
        remote(mine, mine, sends.at[2], recvs.at[2], {"row": lax.rem(at.row + d, rows)}).start()
    line = lined.at[pl.ds(0, rows - 1)]
    await_bytes(line, recvs.at[2])

    def across(d):
        return remote(lined, out.at[at.core, here], sends.at[3], plane_recv.at[d], beside(d))

    each(1, plane, lambda d: across(d).start())
    remote(lined, out.at[at.core, here], sends.at[4], recvs.at[4], sibling).start()
    out[at.core, here] = lined[...]

    def forward(d):
        block = out.at[at.core, lax.rem(here - d + plane, plane)]
        remote(lined, block, sends.at[3], plane_recv.at[d], beside(d)).wait_recv()
        remote(block, block, sends.at[4], recvs.at[4], sibling).start()

    each(1, plane, forward)
    await_bytes(out.at[0], recvs.at[4])
    left += [(line, sends.at[2]), (out.at[0, pl.ds(0, plane - 1)], sends.at[3]), (out.at[0], sends.at[4])]
    for ref, semaphore in left:
        await_bytes(ref, semaphore)


def finish_kernel(
    rows, cols, counts, forces, pos, vel, acc, jerk, step, new_pos, new_vel, new_acc, new_jerk, total, lined
):
    at = Place(rows, cols)
    width = pos.shape[1]
    highs = width // LANES
    mine = at.row * cols + at.col
    features = (0, 1, 2, 4, 5, 6)
    share = forces.shape[3]
    together = 8
    at8 = lax.broadcasted_iota(jnp.int32, (highs, LANES), 0)
    at_low = lax.broadcasted_iota(jnp.int32, (LANES, LANES), 0)
    total[...] = jnp.zeros_like(total)

    def one(n, carry):
        t, first = n // (PARTS // together), lax.rem(n, PARTS // together) * together
        lefts, rights = [], []
        for k in range(together):
            member = first + k
            spots = []
            for b in range(2):
                cube = (2 * t + b) // share
                quarter = cube // at.layers
                z = lax.rem(cube, at.layers) * 2 + member // 8
                y = quarter // at.half * 2 + lax.rem(member // 4, 2)
                x = lax.rem(quarter, at.half) * 2 + lax.rem(member // 2, 2)
                spots.append((lax.rem(member, 2), y * at.side + x, z, lax.rem(2 * t + b, share)))
            star = forces[(*spots[0], slice(3, 4), slice(None))].astype(jnp.int32)
            ok = (star >= 0) & (star // width == mine)
            place = lax.rem(star, width)
            here = jnp.where(ok, place // LANES, -1) == at8
            low = lax.rem(place, LANES)
            rights.append(jnp.where(at_low == low, 1.0, 0.0).astype(BF16))
            pieces = [[], [], []]
            for f in features:
                row = forces[(*spots[f // 4], slice(f % 4, f % 4 + 1), slice(None))]
                for p, piece in enumerate(split3(jnp.where(here, row, 0.0))):
                    pieces[p].append(piece)
            flag = jnp.where(here, 1.0, 0.0)
            blank = jnp.zeros_like(flag)
            lefts.append(jnp.concatenate(pieces[0] + pieces[1] + pieces[2] + [flag, blank], 0).astype(BF16))
        left = jnp.concatenate(lefts, 1)
        right = jnp.concatenate(rights, 1)
        total[...] += lax.dot_general(left, right, (((1,), (1,)), ((), ())), preferred_element_type=F32)
        return carry

    live = lax.fori_loop(0, rows, lambda q, n: n + counts[q, 1, 0], 0)
    lax.fori_loop(0, (live + PARTS - 1) // PARTS * (PARTS // together), one, 0)

    for order in range(7):
        if order < 6:
            parts = [total[(p * 6 + order) * highs : (p * 6 + order + 1) * highs, :] for p in range(3)]
            plane = parts[0] + parts[1] + parts[2]
        else:
            plane = total[18 * highs : 19 * highs, :]
        for c in range(highs):
            lined[order : order + 1, c * LANES : (c + 1) * LANES] = plane[c : c + 1, :]

    on = lined[6:7, :] > 0.5
    a1, k1 = lined[0:3, :], lined[3:6, :]
    x, v, a, k, dt = pos[...], vel[...], acc[...], jerk[...], step[...]
    v1 = v + 0.5 * dt * (a + a1) + dt * dt / 12.0 * (k - k1)
    x1 = x + 0.5 * dt * (v + v1) + dt * dt / 12.0 * (a - a1)
    new_pos[...] = jnp.where(on, x1, x)
    new_vel[...] = jnp.where(on, v1, v)
    new_acc[...] = jnp.where(on, a1, a)
    new_jerk[...] = jnp.where(on, k1, k)


def params(collective_id=None, limit=32 * 2**20):
    if collective_id is None:
        return pltpu.CompilerParams(vmem_limit_bytes=limit)
    return pltpu.CompilerParams(collective_id=collective_id, has_side_effects=True, vmem_limit_bytes=limit)


def per_device(positions, velocities, accels, jerks, masses, elapsed, active, live_tiles):
    rows = lax.axis_size("row")
    cols = lax.axis_size("col")
    width = positions.shape[1]
    tiles = active.shape[0] // TILE
    unit = TILE // PARTS
    blocks = 2 * rows
    cubes = rows * cols // PARTS
    share = blocks // cubes
    plane = cols // 2
    total_stars = width * rows * cols

    live = jnp.arange(tiles)[:, None] < live_tiles[0]
    named = jnp.where(live, active.reshape(tiles, TILE), -1)
    parts = named.reshape(tiles, PARTS, unit).transpose(1, 0, 2).reshape(PARTS, 1, LANES)
    msg = jnp.concatenate([parts, jnp.broadcast_to(live_tiles[0], parts.shape)], 1)

    quarters, layers = cols // 8, rows // 2
    cube_scratch = [
        VMEM((blocks, 4, LANES), F32),
        VMEM((quarters, layers * share, 4, LANES), F32),
        VMEM((layers, share, 4, LANES), F32),
    ]
    dma = pltpu.SemaphoreType.DMA

    ids, states, j_side, j_mass = pl.pallas_call(
        functools.partial(gather_kernel, rows, cols, total_stars),
        out_shape=(
            jax.ShapeDtypeStruct((rows, 2, LANES), jnp.int32),
            jax.ShapeDtypeStruct((blocks, 4, LANES), F32),
            jax.ShapeDtypeStruct((PARTS * width, LANES), BF16),
            jax.ShapeDtypeStruct((32, PARTS * width), BF16),
        ),
        in_specs=[vmem()] * 7,
        out_specs=(vmem(),) * 4,
        scratch_shapes=[VMEM((PARTS, 8, width), F32)]
        + cube_scratch
        + [VMEM((6 * PARTS * width // LANES, 3 * LANES), BF16), dma((6,)), dma((6,))],
        compiler_params=params(0),
        name="gather_states",
    )(positions, velocities, accels, jerks, masses, elapsed, msg)

    pair_count = rows * LANES * PARTS * width
    partial = pl.pallas_call(
        functools.partial(sweep_kernel, rows, cols),
        out_shape=jax.ShapeDtypeStruct((blocks, 4, LANES), F32),
        in_specs=[smem()] + [vmem()] * 4,
        out_specs=vmem(),
        scratch_shapes=[VMEM((rows + 2, 8, LANES), F32)],
        compiler_params=params(),
        cost_estimate=pl.CostEstimate(flops=200 * pair_count, bytes_accessed=2**20, transcendentals=pair_count),
        name="pair_sums",
    )(ids, ids, states, j_side, j_mass)

    forces = pl.pallas_call(
        functools.partial(deliver_kernel, rows, cols),
        out_shape=jax.ShapeDtypeStruct((2, plane, rows, share, 4, LANES), F32),
        in_specs=[vmem()],
        out_specs=vmem(),
        scratch_shapes=cube_scratch + [VMEM((rows, share, 4, LANES), F32), dma((5,)), dma((5,)), dma((plane,))],
        compiler_params=params(1),
        name="deliver_forces",
    )(partial)

    return pl.pallas_call(
        functools.partial(finish_kernel, rows, cols),
        out_shape=tuple(jax.ShapeDtypeStruct((3, width), F32) for _ in range(4)),
        in_specs=[smem()] + [vmem()] * 6,
        out_specs=(vmem(),) * 4,
        scratch_shapes=[VMEM((20 * width // LANES, LANES), F32), VMEM((8, width), F32)],
        compiler_params=params(),
        name="finish_step",
    )(ids, forces, positions, velocities, accels, jerks, elapsed)


def solution(mesh):
    stars = P(None, ("row", "col"))
    in_specs = (stars,) * 6 + (P("row"), P("row"))
    return jax.shard_map(per_device, mesh=mesh, in_specs=in_specs, out_specs=(stars,) * 4, check_vma=False)
```

time: 165 us -> 141 us (0.85)
  Pallas kernels: 161 us -> 134 us
  local copies, waits for them, and re-layouts: 1.67 us -> 5.24 us
    pallas_call x2 -> x0, Pallas kernels: 30.6 us -> none  [the longest x1 27.2 us: per_device(): pl.pallas_call(functools.partial(cube_sum_kernel, rows, cols), out_shape=...]
    pallas_call x1, Pallas kernels: 23.8 us -> 49.6 us  [per_device(): pl.pallas_call(functools.partial(gather_kernel, rows, cols, total_stars),...]
    pallas_call x1, Pallas kernels: 61.2 us -> 37.8 us  [per_device(): pl.pallas_call(functools.partial(sweep_kernel, rows, cols), out_shape=jax...]
    unnamed x12 -> x22, local copies, waits for them, and re-layouts: 0.72 us -> 4.27 us
where the time goes in v2:
time: 141 us; the launch traced here: 140 us
  Pallas kernels  134 us (95%)
  local copies, waits for them, and re-layouts  5.24 us (4%)
  between operations  1.43 us (1%)
    pallas_call x1, Pallas kernels, per_device(): pl.pallas_call(functools.partial(gather_kernel, rows, cols, total_stars),...  49.6 us
    pallas_call x1, Pallas kernels, per_device(): pl.pallas_call(functools.partial(deliver_kernel, rows, cols), out_shape=j...  40 us
    pallas_call x1, Pallas kernels, per_device(): pl.pallas_call(functools.partial(sweep_kernel, rows, cols), out_shape=jax...  37.8 us
    pallas_call x1, Pallas kernels, per_device(): pl.pallas_call(functools.partial(finish_kernel, rows, cols), out_shape=tu...  6.26 us
    unnamed x22, local copies, waits for them, and re-layouts  4.27 us

profile of v2, /device:TPU:1, one launch (start us, length us, event | category | flops | bytes accessed | tf_op | source)
XLA Modules:
  0.0 140.5 jit_solution(4133821592763561773)
XLA Ops:
  1.3 0.8 reshape.26
  2.1 0.1 select_bitcast_fusion
  2.2 0.1 copy.12
  2.3 0.1 copy.13
  2.4 0.0 copy-start
  2.4 0.7 copy-done
  3.1 0.0 copy-start.2
  3.1 0.7 copy-done.2
  3.8 0.0 copy-start.4
  3.8 0.7 copy-done.4
  4.5 0.0 copy-start.6
  4.5 0.7 copy-done.6
  5.2 0.0 copy-start.8
  5.2 0.7 copy-done.8
  5.9 0.0 copy-start.10
  5.9 0.7 copy-done.10
  6.6 49.6 %gather_states.1 = (s32[16,2,128]{2,1,0:T(2,128)S(1)}, f32[32,4,128]{2,1,0:T(4,128)S(1)}, bf16[16384,128]{1,0:T(8,128)(2,1)S(1)}, bf16[32,16384]{1,0:T(8,128)(2,1)S(1)}) custom-call(f32[3,1024]{1,0:T(4,128)S(1)} %copy-done, f32[3,1024]{1,0:T(4,128)S(1)} %copy-done.2, f32[3,1024]{1,0:T(4,128)S(1)} %copy-done.4, f32[3,1024]{1,0:T(4,128)S(1)} %copy-done.6, ...), custom_call_target="tpu_custom_call" | custom-call | tf_op jit(solution)/shard_map/gather_states/pallas_call | solution.py:513
  56.2 0.0 copy-start.1
  56.2 0.0 copy-start.3
  56.2 0.0 copy-start.5
  56.3 0.0 copy-start.7
  56.3 0.0 copy-start.9
  56.3 37.8 %pair_sums.1.partial = f32[32,4,128]{2,1,0:T(4,128)S(1)} custom-call(s32[16,2,128]{2,1,0:T(2,128)S(1)} %get-tuple-element.8.counts.ids, s32[16,2,128]{2,1,0:T(2,128)S(1)} %get-tuple-element.8.counts.ids, f32[32,4,128]{2,1,0:T(4,128)S(1)} %get-tuple-element.9.states, bf16[16384,128]{1,0:T(8,128)(2,1)S(1)} %get-tuple-element.10.j_side, ...), custom_call_target="tpu_custom_call" | custom-call | flops 6710886400 | bytes 1048576 | tf_op jit(solution)/shard_map/pair_sums/pallas_call | solution.py:531
  94.1 40.0 %deliver_forces.1.forces = f32[2,16,16,1,4,128]{5,4,3,2,1,0:T(4,128)S(1)} custom-call(f32[32,4,128]{2,1,0:T(4,128)S(1)} %pair_sums.1.partial), custom_call_target="tpu_custom_call" | custom-call | tf_op jit(solution)/shard_map/deliver_forces/pallas_call | solution.py:542
  134.2 0.0 copy-done.1
  134.2 0.0 copy-done.3
  134.2 0.0 copy-done.5
  134.2 0.0 copy-done.7
  134.2 0.0 copy-done.9
  134.2 6.3 %finish_step.1 = (f32[3,1024]{1,0:T(4,128)}, f32[3,1024]{1,0:T(4,128)}, f32[3,1024]{1,0:T(4,128)}, f32[3,1024]{1,0:T(4,128)}) custom-call(s32[16,2,128]{2,1,0:T(2,128)S(1)} %get-tuple-element.8.counts.ids, f32[2,16,16,1,4,128]{5,4,3,2,1,0:T(4,128)S(1)} %deliver_forces.1.forces, f32[3,1024]{1,0:T(4,128)S(1)} %copy-done.1, f32[3,1024]{1,0:T(4,128)S(1)} %copy-done.3, ...), custom_call_target="tpu_custom_call" | custom-call | tf_op jit(solution)/shard_map/finish_step/pallas_call | solution.py:552
  (2 shorter events, 0.0 us)
Async XLA Ops:
  2.4 0.7 copy-start
  3.1 0.7 copy-start.2
  3.8 0.7 copy-start.4
  4.5 0.7 copy-start.6
  5.2 0.7 copy-start.8
  5.9 0.7 copy-start.10
  56.2 77.9 %copy-start.1 = (f32[3,1024]{1,0:T(4,128)S(1)}, f32[3,1024]{1,0:T(4,128)}, u32[]{:S(2)}) copy-start(f32[3,1024]{1,0:T(4,128)} %pos.3) | copy-start | bytes 36868
  56.2 77.9 %copy-start.3 = (f32[3,1024]{1,0:T(4,128)S(1)}, f32[3,1024]{1,0:T(4,128)}, u32[]{:S(2)}) copy-start(f32[3,1024]{1,0:T(4,128)} %vel.3) | copy-start | bytes 36868
  56.2 77.9 %copy-start.5 = (f32[3,1024]{1,0:T(4,128)S(1)}, f32[3,1024]{1,0:T(4,128)}, u32[]{:S(2)}) copy-start(f32[3,1024]{1,0:T(4,128)} %acc.3) | copy-start | bytes 36868
  56.3 77.9 %copy-start.7 = (f32[3,1024]{1,0:T(4,128)S(1)}, f32[3,1024]{1,0:T(4,128)}, u32[]{:S(2)}) copy-start(f32[3,1024]{1,0:T(4,128)} %jerk.3) | copy-start | bytes 36868
  56.3 77.9 %copy-start.9 = (f32[1,1024]{1,0:T(1,128)S(1)}, f32[1,1024]{1,0:T(1,128)}, u32[]{:S(2)}) copy-start(f32[1,1024]{1,0:T(1,128)} %step.3) | copy-start | bytes 12292

commit v3 on v2

v3 whole, which is shorter than its diff:
```python
import functools

import jax
import jax.numpy as jnp
from jax import lax
from jax.experimental import pallas as pl
from jax.experimental.pallas import tpu as pltpu
from jax.sharding import PartitionSpec as P

TILE = 128
EPS2 = 0.01
LANES = 128
BLOCK_J = 4096
PIECE_J = 256
PARTS = 16
MESH = pl.DeviceIdType.MESH
VMEM = pltpu.VMEM
F32 = jnp.float32
BF16 = jnp.bfloat16


def anywhere():
    return pl.BlockSpec(memory_space=pl.ANY)


def vmem():
    return pl.BlockSpec(memory_space=pltpu.VMEM)


def smem():
    return pl.BlockSpec(memory_space=pltpu.SMEM)


def split3(x):
    high = x.astype(BF16).astype(F32)
    rest = x - high
    mid = rest.astype(BF16).astype(F32)
    return high, mid, rest - mid


class Place:
    def __init__(self, rows, cols):
        self.rows, self.cols = rows, cols
        self.side = {32: 4, 8: 2, 2: 1}[cols]
        self.plane, self.layers = self.side * self.side, rows // 2
        self.groups = 2 * self.plane
        self.row = lax.axis_index("row")
        self.col = lax.axis_index("col")
        self.spot, self.core = self.col // 2, lax.rem(self.col, 2)
        self.parity, self.layer = lax.rem(self.row, 2), self.row // 2
        self.group = self.parity * self.plane + self.spot
        self.member = self.layer * 2 + self.core
        self.sibling = {"col": self.spot * 2 + 1 - self.core}
        self.twin = {"row": self.layer * 2 + 1 - self.parity}

    def in_layer(self, layer):
        return {"row": layer * 2 + self.parity}

    def at_spot(self, spot):
        return {"col": spot * 2 + self.core}


def signal(device):
    pl.semaphore_signal(pltpu.get_barrier_semaphore(), inc=1, device_id=device, device_id_type=MESH)


def await_greetings(count):
    pl.semaphore_wait(pltpu.get_barrier_semaphore(), count)


def each(first, last, body, step=1):
    def one(n, carry):
        body(first + n * step)
        return carry

    lax.fori_loop(0, (last - first + step - 1) // step, one, 0)


def remote(source, target, send, recv, device):
    return pltpu.make_async_remote_copy(
        src_ref=source, dst_ref=target, send_sem=send, recv_sem=recv, device_id=device, device_id_type=MESH
    )


def await_bytes(ref, semaphore):
    pltpu.make_async_copy(ref, ref, semaphore).wait()


def dots(tile):
    first = lax.broadcasted_iota(jnp.int32, tile.shape, 0) < 3
    swapped = pltpu.roll(tile, 4, 0)
    norm = jnp.sum(jnp.where(first, tile * tile, 0.0), axis=0, keepdims=True)
    cross = jnp.sum(jnp.where(first, tile * swapped, 0.0), axis=0, keepdims=True)
    return norm, cross


def group_sums(at, blocks, from_twin, from_spots, sends, recvs, meanwhile=None):
    share = blocks.shape[0] // at.groups
    span = share * at.plane
    theirs = blocks.at[pl.ds((1 - at.parity) * span, span)]
    remote(theirs, from_twin, sends.at[0], recvs.at[0], at.twin).start()
    mine = pl.ds(at.parity * span, span)
    await_bytes(from_twin, recvs.at[0])
    blocks[mine] = blocks[mine] + from_twin[...]
    from_spots[at.spot] = blocks[pl.ds(at.group * share, share)]

    def to_spot(d):
        spot = lax.rem(at.spot + d, at.plane)
        part = blocks.at[pl.ds(at.parity * span + spot * share, share)]
        remote(part, from_spots.at[at.spot], sends.at[1], recvs.at[1], at.at_spot(spot)).start()

    left = [(from_twin, sends.at[0])]
    if at.plane > 1:
        for d in range(1, at.plane):
            to_spot(d)
        if meanwhile is not None:
            meanwhile()
        rest = from_spots.at[pl.ds(0, at.plane - 1)]
        await_bytes(rest, recvs.at[1])
        left.append((rest, sends.at[1]))
    elif meanwhile is not None:
        meanwhile()
    return jnp.sum(from_spots[...], axis=0), left


def gather_kernel(
    rows,
    cols,
    total_stars,
    pos_in,
    vel_in,
    acc_in,
    jerk_in,
    mass_in,
    step_in,
    msg,
    ids,
    states,
    j_side,
    j_mass,
    shard,
    picked,
    from_twin,
    from_spots,
    table,
    pos,
    vel,
    acc,
    jerk,
    mass,
    step,
    loads,
    sends,
    recvs,
    id_send,
    id_recv,
    right_recv,
    left_recv,
    core_recv,
):
    at = Place(rows, cols)
    me, mine, layers = at.member, at.group, at.layers
    share = states.shape[0] // at.groups
    pairs = ((pos_in, pos), (vel_in, vel), (acc_in, acc), (jerk_in, jerk), (mass_in, mass), (step_in, step))
    loading = [pltpu.make_async_copy(source, target, loads.at[n]) for n, (source, target) in enumerate(pairs)]
    for load in loading:
        load.start()
    signal(at.sibling)
    for d in range(1, rows):
        signal({"row": lax.rem(at.row + d, rows)})
    for d in range(1, at.plane):
        signal(at.at_spot(lax.rem(at.spot + d, at.plane)))
    ids[at.row] = msg[me]
    for load in loading:
        load.wait()
    dt = step[...]
    a, j, v = acc[...], jerk[...], vel[...]
    shard[me, 0:3, :] = pos[...] + dt * (v + dt * (0.5 * a + dt * j / 6.0))
    shard[me, 3:4, :] = mass[...] / total_stars
    shard[me, 4:7, :] = v + dt * (a + dt * (0.5 * j))
    shard[me, 7:8, :] = jnp.ones_like(dt)
    await_greetings(rows + at.plane - 1)

    width = pos.shape[1]
    chunks = width // LANES

    def prepare(z):
        tile = shard[z]
        norm, cross = dots(tile)
        h, m, l = split3(tile)
        pieces = split3(norm) + split3(cross)
        line = lax.broadcasted_iota(jnp.int32, tile.shape, 0)
        extra = jnp.zeros_like(tile)
        for n, piece in enumerate(pieces):
            extra = jnp.where(line == n, piece, extra)
        blank = jnp.zeros((LANES - 56, width), F32)
        side = jnp.concatenate([h, h, h, m, m, l, extra, blank], 0)
        for c in range(chunks):
            place = pl.ds(pl.multiple_of(z * width + c * LANES, LANES), LANES)
            j_side[place, :] = side[:, c * LANES : (c + 1) * LANES].T.astype(BF16)
        h, m, l = split3(tile * tile[3:4, :])
        place = pl.ds(pl.multiple_of(z * width, width), width)
        j_mass[:, place] = jnp.concatenate([h, m, l, jnp.zeros_like(tile)], 0).astype(BF16)

    def prepare_layers(s, both):
        def one(n):
            layer = lax.rem(at.layer + (n // 2 * 2 - 1) * s + layers, layers)
            prepare(layer * 2 + lax.rem(n, 2))

        each(0, 4 if both else 2, one)

    def ring(s, way):
        block = shard.at[lax.rem(at.layer - way * s + layers, layers) * 2 + at.core]
        recv = (right_recv if way > 0 else left_recv).at[s]
        return remote(block, block, sends.at[4], recv, at.in_layer(lax.rem(at.layer + way + layers, layers)))

    def arrived(s, way):
        block = shard.at[lax.rem(at.layer - way * (s + 1) + 2 * layers, layers) * 2 + at.core]
        recv = (right_recv if way > 0 else left_recv).at[s]
        remote(block, block, sends.at[4], recv, at.in_layer(lax.rem(at.layer + way + layers, layers))).wait_recv()

    def across(s, way, core):
        block = shard.at[lax.rem(at.layer - way * s + layers, layers) * 2 + core]
        return remote(block, block, sends.at[5], core_recv.at[2 * s + (1 - way) // 2], at.sibling)

    ways = (layers // 2, layers - 1 - layers // 2)
    for s in range(ways[0] + 1):
        if s < ways[0]:
            ring(s, 1).start()
        if s < ways[1]:
            ring(s, -1).start()
        across(s, 1, at.core).start()
        if 0 < s <= ways[1]:
            across(s, -1, at.core).start()
        if s == 0:

            def send_ids(d):
                peer = lax.rem(at.row + d, rows)
                part = msg.at[peer // 2 * 2 + at.core]
                remote(part, ids.at[at.row], id_send, id_recv, {"row": peer}).start()

            each(1, rows, send_ids)
        else:
            across(s - 1, 1, 1 - at.core).wait_recv()
            if 0 < s - 1 <= ways[1]:
                across(s - 1, -1, 1 - at.core).wait_recv()
            if s < ways[0]:
                prepare_layers(s - 1, 0 < s - 1 <= ways[1])
        if s < ways[0]:
            arrived(s, 1)
        if s < ways[1]:
            arrived(s, -1)
    across(ways[0], 1, 1 - at.core).wait_recv()
    id_rest = ids.at[pl.ds(0, rows - 1)]
    await_bytes(id_rest, id_recv)

    high_count = PARTS * chunks
    features = (0, 1, 2, 4, 5, 6)
    groups = min(4, rows)
    for order, f in enumerate(features):
        plane = jnp.concatenate([shard[:, f, c * LANES : (c + 1) * LANES] for c in range(chunks)], 0)
        h, m, l = split3(plane)
        table[order * high_count : (order + 1) * high_count, :] = jnp.concatenate([h, m, l], 1).astype(BF16)
    picked[...] = jnp.zeros_like(picked)

    def part(g, carry):
        first = g * groups
        star = jnp.concatenate([ids[first + n, 0:1, :] for n in range(groups)], 1)
        owner = star // width
        row, col = owner // cols, lax.rem(owner, cols)
        group = lax.rem(row, 2) * at.plane + col // 2
        member = row // 2 * 2 + lax.rem(col, 2)
        place = lax.rem(star, width)
        high = jnp.where((star >= 0) & (group == mine), place // LANES * PARTS + member, -1)
        low = lax.rem(place, LANES)
        span = groups * LANES
        pick = jnp.where(lax.broadcasted_iota(jnp.int32, (LANES, span), 0) == low, 1.0, 0.0).astype(BF16)
        pick = jnp.concatenate([pick, pick, pick], 0)
        at_row = lax.broadcasted_iota(jnp.int32, (high_count, span), 0) == high
        for order, f in enumerate(features):
            values = jnp.dot(table[order * high_count : (order + 1) * high_count, :], pick, preferred_element_type=F32)
            found = jnp.sum(jnp.where(at_row, values, 0.0), axis=0, keepdims=True)
            for n in range(groups):
                picked[2 * (first + n) + f // 4, f % 4 : f % 4 + 1, :] = found[:, n * LANES : (n + 1) * LANES]
        return carry

    lax.fori_loop(0, rows // groups, part, 0)

    late = ways[0] - 1

    def first_rest():
        prepare_layers(late, 0 < late <= ways[1])

    total, left = group_sums(at, picked, from_twin, from_spots, sends, recvs, first_rest)
    own = pl.ds(mine * share, share)
    states[own] = total
    span = at.plane * share
    half = pl.ds(at.parity * span, span)
    for d in range(1, at.plane):
        spot = lax.rem(at.spot + d, at.plane)
        remote(states.at[own], states.at[own], sends.at[2], recvs.at[2], at.at_spot(spot)).start()
    prepare_layers(ways[0], False)
    if at.plane > 1:
        rest = states.at[pl.ds(0, span - share)]
        await_bytes(rest, recvs.at[2])
        left.append((rest, sends.at[2]))
    remote(states.at[half], states.at[half], sends.at[3], recvs.at[3], at.twin).start()
    await_bytes(states.at[half], recvs.at[3])
    left += [
        (states.at[half], sends.at[3]),
        (shard.at[pl.ds(0, layers - 1)], sends.at[4]),
        (shard.at[pl.ds(0, layers)], sends.at[5]),
        (id_rest, id_send),
    ]
    for ref, semaphore in left:
        await_bytes(ref, semaphore)


def sweep_kernel(rows, cols, counts, ids, states, j_side, j_mass, out, i_tiles):
    at = Place(rows, cols)
    total = j_side.shape[0]
    at8 = lax.broadcasted_iota(jnp.int32, (8, LANES), 0)
    lane = lax.broadcasted_iota(jnp.int32, (8, LANES), 1)
    out[...] = jnp.zeros_like(out)
    i_tiles[...] = jnp.where(lax.broadcasted_iota(jnp.int32, i_tiles.shape, 1) == 3, -1.0, 0.0)

    def pack(q, offset):
        tile = jnp.concatenate([states[2 * q], states[2 * q + 1]], 0)
        tile = jnp.where(at8 == 3, ids[q, 0:1, :].astype(F32), tile)
        t, shift = offset // LANES, lax.rem(offset, LANES)
        rolled = pltpu.roll(tile, shift, 1)
        i_tiles[t] = jnp.where(lane >= shift, rolled, i_tiles[t])
        i_tiles[t + 1] = jnp.where(lane < shift, rolled, i_tiles[t + 1])
        return offset + counts[q, 1, 0] * (TILE // PARTS)

    used = lax.fori_loop(0, rows, pack, 0)

    def right_of(tile):
        norm, cross = dots(tile)
        h, m, l = split3(tile)
        nh, nm, nl = split3(norm + EPS2)
        ch, cm, cl = split3(cross)

        def for_r(piece, last):
            return jnp.where(at8 < 3, -2.0 * piece, jnp.where(at8 == 7, last, 0.0))

        def for_b(piece, last):
            return jnp.where(at8 == 7, last, jnp.where(at8 == 3, 0.0, -pltpu.roll(piece, 4, 0)))

        r_extra = jnp.where(at8 < 3, 1.0, 0.0)
        b_extra = jnp.where((at8 >= 3) & (at8 < 6), 1.0, 0.0)
        blank = jnp.zeros((LANES - 56, LANES), F32)
        right_r = jnp.concatenate(
            [for_r(h, nh), for_r(m, nm), for_r(l, nl), for_r(h, 0.0), for_r(m, 0.0), for_r(h, 0.0), r_extra, blank], 0
        )
        right_b = jnp.concatenate(
            [for_b(h, ch), for_b(m, cm), for_b(l, cl), for_b(h, 0.0), for_b(m, 0.0), for_b(h, 0.0), b_extra, blank], 0
        )
        return jnp.concatenate([right_r, right_b], 1).astype(BF16)

    def run(t, carry):
        tile = i_tiles[t]
        right = right_of(tile)

        def one_block(n, sums):
            def place(s):
                return pl.ds(pl.multiple_of(n * BLOCK_J + s * PIECE_J, PIECE_J), PIECE_J)

            def distances(s):
                return jnp.dot(j_side[place(s), :], right, preferred_element_type=F32)

            ahead = distances(0)
            for s in range(BLOCK_J // PIECE_J):
                both = ahead
                if s + 1 < BLOCK_J // PIECE_J:
                    ahead = distances(s + 1)
                inverse = lax.rsqrt(both[:, 0:LANES])
                square = inverse * inverse
                near = square * inverse
                tilt = near * square * both[:, LANES:]
                pair = jnp.concatenate([near, tilt], 1)
                high = pair.astype(BF16)
                low = (pair - high.astype(F32)).astype(BF16)
                weights = j_mass[:, place(s)]
                sums += jnp.dot(
                    jnp.concatenate([weights, weights], 1),
                    jnp.concatenate([high, low], 0),
                    preferred_element_type=F32,
                )
            return sums

        sums = lax.fori_loop(0, total // BLOCK_J, one_block, jnp.zeros((32, 2 * LANES), F32))
        sums = sums[0:8] + sums[8:16] + sums[16:24]
        near, tilt = sums[:, 0:LANES], sums[:, LANES:]
        near = near - tile * near[7:8]
        tilt = tilt - tile * tilt[7:8]
        force = near - jnp.where(at8 >= 4, 3.0 * pltpu.roll(tilt, 4, 0), 0.0)
        star = tile[3:4]
        force = jnp.where(star >= 0, force, 0.0)
        force = jnp.where(at8 == 3, jnp.where(at.group == 0, star, 0.0), force)
        out[2 * t] = force[0:4]
        out[2 * t + 1] = force[4:8]
        return carry

    lax.fori_loop(0, (used + LANES - 1) // LANES, run, 0)


def deliver_kernel(rows, cols, partial, out, blocks, from_twin, from_spots, lined, sends, recvs, plane_recv):
    at = Place(rows, cols)
    plane = at.plane
    signal(at.sibling)
    for d in range(1, rows):
        signal({"row": lax.rem(at.row + d, rows)})
    for d in range(1, plane):
        signal(at.at_spot(lax.rem(at.spot + d, plane)))
    blocks[...] = partial[...]
    await_greetings(rows + plane - 1)

    total, left = group_sums(at, blocks, from_twin, from_spots, sends, recvs)
    lined[at.row] = total
    mine = lined.at[at.row]
    for d in range(1, rows):
        remote(mine, mine, sends.at[2], recvs.at[2], {"row": lax.rem(at.row + d, rows)}).start()
    line = lined.at[pl.ds(0, rows - 1)]
    await_bytes(line, recvs.at[2])

    def across(d):
        spot = lax.rem(at.spot + d, plane)
        return remote(lined, out.at[at.core, at.spot], sends.at[3], plane_recv.at[d], at.at_spot(spot))

    for d in range(1, plane):
        across(d).start()
    remote(lined, out.at[at.core, at.spot], sends.at[4], recvs.at[4], at.sibling).start()
    out[at.core, at.spot] = lined[...]
    for d in range(1, plane):
        block = out.at[at.core, lax.rem(at.spot - d + plane, plane)]
        remote(lined, block, sends.at[3], plane_recv.at[d], at.sibling).wait_recv()
        remote(block, block, sends.at[4], recvs.at[4], at.sibling).start()
    await_bytes(out.at[0], recvs.at[4])
    left += [(line, sends.at[2]), (out.at[0], sends.at[4])]
    if plane > 1:
        left.append((out.at[0, pl.ds(0, plane - 1)], sends.at[3]))
    for ref, semaphore in left:
        await_bytes(ref, semaphore)


def finish_kernel(
    rows,
    cols,
    counts,
    forces,
    pos_in,
    vel_in,
    acc_in,
    jerk_in,
    step_in,
    new_pos,
    new_vel,
    new_acc,
    new_jerk,
    total,
    lined,
    pos,
    vel,
    acc,
    jerk,
    step,
    loads,
):
    at = Place(rows, cols)
    pairs = ((pos_in, pos), (vel_in, vel), (acc_in, acc), (jerk_in, jerk), (step_in, step))
    loading = [pltpu.make_async_copy(source, target, loads.at[n]) for n, (source, target) in enumerate(pairs)]
    for load in loading:
        load.start()
    width = pos.shape[1]
    highs = width // LANES
    mine = at.row * cols + at.col
    features = (0, 1, 2, 4, 5, 6)
    share = forces.shape[3]
    together = 8
    at8 = lax.broadcasted_iota(jnp.int32, (highs, LANES), 0)
    at_low = lax.broadcasted_iota(jnp.int32, (LANES, LANES), 0)
    total[...] = jnp.zeros_like(total)

    def one(n, carry):
        t, first = n // (PARTS // together), lax.rem(n, PARTS // together) * together
        lefts, rights = [], []
        for k in range(together):
            member = first + k
            spots = []
            for b in range(2):
                group = (2 * t + b) // share
                z = member // 2 * 2 + group // at.plane
                spots.append((lax.rem(member, 2), lax.rem(group, at.plane), z, lax.rem(2 * t + b, share)))
            star = forces[(*spots[0], slice(3, 4), slice(None))].astype(jnp.int32)
            ok = (star >= 0) & (star // width == mine)
            place = lax.rem(star, width)
            here = jnp.where(ok, place // LANES, -1) == at8
            low = lax.rem(place, LANES)
            rights.append(jnp.where(at_low == low, 1.0, 0.0).astype(BF16))
            pieces = [[], [], []]
            for f in features:
                row = forces[(*spots[f // 4], slice(f % 4, f % 4 + 1), slice(None))]
                for p, piece in enumerate(split3(jnp.where(here, row, 0.0))):
                    pieces[p].append(piece)
            flag = jnp.where(here, 1.0, 0.0)
            blank = jnp.zeros_like(flag)
            lefts.append(jnp.concatenate(pieces[0] + pieces[1] + pieces[2] + [flag, blank], 0).astype(BF16))
        left = jnp.concatenate(lefts, 1)
        right = jnp.concatenate(rights, 1)
        total[...] += lax.dot_general(left, right, (((1,), (1,)), ((), ())), preferred_element_type=F32)
        return carry

    live = lax.fori_loop(0, rows, lambda q, n: n + counts[q, 1, 0], 0)
    lax.fori_loop(0, (live + PARTS - 1) // PARTS * (PARTS // together), one, 0)

    for order in range(7):
        if order < 6:
            parts = [total[(p * 6 + order) * highs : (p * 6 + order + 1) * highs, :] for p in range(3)]
            plane = parts[0] + parts[1] + parts[2]
        else:
            plane = total[18 * highs : 19 * highs, :]
        for c in range(highs):
            lined[order : order + 1, c * LANES : (c + 1) * LANES] = plane[c : c + 1, :]

    for load in loading:
        load.wait()
    on = lined[6:7, :] > 0.5
    a1, k1 = lined[0:3, :], lined[3:6, :]
    x, v, a, k, dt = pos[...], vel[...], acc[...], jerk[...], step[...]
    v1 = v + 0.5 * dt * (a + a1) + dt * dt / 12.0 * (k - k1)
    x1 = x + 0.5 * dt * (v + v1) + dt * dt / 12.0 * (a - a1)
    new_pos[...] = jnp.where(on, x1, x)
    new_vel[...] = jnp.where(on, v1, v)
    new_acc[...] = jnp.where(on, a1, a)
    new_jerk[...] = jnp.where(on, k1, k)


def params(collective_id=None, limit=32 * 2**20):
    if collective_id is None:
        return pltpu.CompilerParams(vmem_limit_bytes=limit)
    return pltpu.CompilerParams(collective_id=collective_id, has_side_effects=True, vmem_limit_bytes=limit)


def per_device(positions, velocities, accels, jerks, masses, elapsed, active, live_tiles):
    rows = lax.axis_size("row")
    cols = lax.axis_size("col")
    width = positions.shape[1]
    tiles = active.shape[0] // TILE
    unit = TILE // PARTS
    blocks = 2 * rows
    plane, layers = cols // 2, rows // 2
    share = blocks // (2 * plane)
    total_stars = width * rows * cols
    dma = pltpu.SemaphoreType.DMA
    triples = [VMEM((3, width), F32) for _ in range(4)]
    single = VMEM((1, width), F32)
    sum_scratch = [
        VMEM((blocks, 4, LANES), F32),
        VMEM((blocks // 2, 4, LANES), F32),
        VMEM((plane, share, 4, LANES), F32),
    ]

    live = jnp.arange(tiles)[:, None] < live_tiles[0]
    named = jnp.where(live, active.reshape(tiles, TILE), -1)
    parts = named.reshape(tiles, PARTS, unit).transpose(1, 0, 2).reshape(PARTS, 1, LANES)
    msg = jnp.concatenate([parts, jnp.broadcast_to(live_tiles[0], parts.shape)], 1)

    ids, states, j_side, j_mass = pl.pallas_call(
        functools.partial(gather_kernel, rows, cols, total_stars),
        out_shape=(
            jax.ShapeDtypeStruct((rows, 2, LANES), jnp.int32),
            jax.ShapeDtypeStruct((blocks, 4, LANES), F32),
            jax.ShapeDtypeStruct((PARTS * width, LANES), BF16),
            jax.ShapeDtypeStruct((32, PARTS * width), BF16),
        ),
        in_specs=[anywhere()] * 6 + [vmem()],
        out_specs=(vmem(),) * 4,
        scratch_shapes=[VMEM((PARTS, 8, width), F32)]
        + sum_scratch
        + [VMEM((6 * PARTS * width // LANES, 3 * LANES), BF16)]
        + triples
        + [single, single, dma((6,)), dma((6,)), dma((4,)), dma, dma]
        + [dma((layers,)), dma((layers,)), dma((2 * layers,))],
        compiler_params=params(0),
        name="gather_states",
    )(positions, velocities, accels, jerks, masses, elapsed, msg)

    pair_count = rows * LANES * PARTS * width
    partial = pl.pallas_call(
        functools.partial(sweep_kernel, rows, cols),
        out_shape=jax.ShapeDtypeStruct((blocks, 4, LANES), F32),
        in_specs=[smem()] + [vmem()] * 4,
        out_specs=vmem(),
        scratch_shapes=[VMEM((rows + 2, 8, LANES), F32)],
        compiler_params=params(),
        cost_estimate=pl.CostEstimate(flops=200 * pair_count, bytes_accessed=2**20, transcendentals=pair_count),
        name="pair_sums",
    )(ids, ids, states, j_side, j_mass)

    forces = pl.pallas_call(
        functools.partial(deliver_kernel, rows, cols),
        out_shape=jax.ShapeDtypeStruct((2, plane, rows, share, 4, LANES), F32),
        in_specs=[vmem()],
        out_specs=vmem(),
        scratch_shapes=sum_scratch + [VMEM((rows, share, 4, LANES), F32), dma((5,)), dma((5,)), dma((plane,))],
        compiler_params=params(1),
        name="deliver_forces",
    )(partial)

    return pl.pallas_call(
        functools.partial(finish_kernel, rows, cols),
        out_shape=tuple(jax.ShapeDtypeStruct((3, width), F32) for _ in range(4)),
        in_specs=[smem(), vmem()] + [anywhere()] * 5,
        out_specs=(vmem(),) * 4,
        scratch_shapes=[VMEM((20 * width // LANES, LANES), F32), VMEM((8, width), F32)] + triples + [single, dma((5,))],
        compiler_params=params(),
        name="finish_step",
    )(ids, forces, positions, velocities, accels, jerks, elapsed)


def solution(mesh):
    stars = P(None, ("row", "col"))
    in_specs = (stars,) * 6 + (P("row"), P("row"))
    return jax.shard_map(per_device, mesh=mesh, in_specs=in_specs, out_specs=(stars,) * 4, check_vma=False)
```

time: 141 us -> 129 us (0.915)
  Pallas kernels: 134 us -> 122 us
    pallas_call x1, Pallas kernels: 40 us -> 31.4 us  [per_device(): pl.pallas_call(functools.partial(deliver_kernel, rows, cols), out_shape=j...]
    pallas_call x1, Pallas kernels: 37.8 us -> 35.4 us  [per_device(): pl.pallas_call(functools.partial(sweep_kernel, rows, cols), out_shape=jax...]
where the time goes in v3:
time: 129 us; the launch traced here: 128 us
  Pallas kernels  122 us (95%)
  local copies, waits for them, and re-layouts  5.24 us (4%)
  between operations  1.43 us (1%)
    pallas_call x1, Pallas kernels, per_device(): pl.pallas_call(functools.partial(gather_kernel, rows, cols, total_stars),...  49.5 us
    pallas_call x1, Pallas kernels, per_device(): pl.pallas_call(functools.partial(sweep_kernel, rows, cols), out_shape=jax...  35.4 us
    pallas_call x1, Pallas kernels, per_device(): pl.pallas_call(functools.partial(deliver_kernel, rows, cols), out_shape=j...  31.4 us
    pallas_call x1, Pallas kernels, per_device(): pl.pallas_call(functools.partial(finish_kernel, rows, cols), out_shape=tu...  5.46 us
    unnamed x22, local copies, waits for them, and re-layouts  4.27 us

profile of v3, /device:TPU:1, one launch (start us, length us, event | category | flops | bytes accessed | tf_op | source)
XLA Modules:
  0.0 128.4 jit_solution(10869999843132569731)
XLA Ops:
  1.3 0.8 reshape.26
  2.1 0.1 select_bitcast_fusion
  2.2 0.1 copy.12
  2.3 0.1 copy.13
  2.4 0.0 copy-start
  2.4 0.7 copy-done
  3.1 0.0 copy-start.2
  3.1 0.7 copy-done.2
  3.8 0.0 copy-start.4
  3.8 0.7 copy-done.4
  4.5 0.0 copy-start.6
  4.5 0.7 copy-done.6
  5.2 0.0 copy-start.8
  5.2 0.7 copy-done.8
  5.9 0.0 copy-start.10
  5.9 0.7 copy-done.10
  6.6 49.5 %gather_states.1 = (s32[16,2,128]{2,1,0:T(2,128)S(1)}, f32[32,4,128]{2,1,0:T(4,128)S(1)}, bf16[16384,128]{1,0:T(8,128)(2,1)S(1)}, bf16[32,16384]{1,0:T(8,128)(2,1)S(1)}) custom-call(f32[3,1024]{1,0:T(4,128)S(1)} %copy-done, f32[3,1024]{1,0:T(4,128)S(1)} %copy-done.2, f32[3,1024]{1,0:T(4,128)S(1)} %copy-done.4, f32[3,1024]{1,0:T(4,128)S(1)} %copy-done.6, ...), custom_call_target="tpu_custom_call" | custom-call | tf_op jit(solution)/shard_map/gather_states/pallas_call | solution.py:569
  56.1 0.0 copy-start.1
  56.1 0.0 copy-start.3
  56.1 0.0 copy-start.5
  56.2 0.0 copy-start.7
  56.2 0.0 copy-start.9
  56.2 35.4 %pair_sums.1.partial = f32[32,4,128]{2,1,0:T(4,128)S(1)} custom-call(s32[16,2,128]{2,1,0:T(2,128)S(1)} %get-tuple-element.8.counts.ids, s32[16,2,128]{2,1,0:T(2,128)S(1)} %get-tuple-element.8.counts.ids, f32[32,4,128]{2,1,0:T(4,128)S(1)} %get-tuple-element.9.states, bf16[16384,128]{1,0:T(8,128)(2,1)S(1)} %get-tuple-element.10.j_side, ...), custom_call_target="tpu_custom_call" | custom-call | flops 6710886400 | bytes 1048576 | tf_op jit(solution)/shard_map/pair_sums/pallas_call | solution.py:590
  91.6 31.4 %deliver_forces.1.forces = f32[2,16,16,1,4,128]{5,4,3,2,1,0:T(4,128)S(1)} custom-call(f32[32,4,128]{2,1,0:T(4,128)S(1)} %pair_sums.1.partial), custom_call_target="tpu_custom_call" | custom-call | tf_op jit(solution)/shard_map/deliver_forces/pallas_call | solution.py:601
  122.9 0.0 copy-done.1
  122.9 0.0 copy-done.3
  122.9 0.0 copy-done.5
  123.0 0.0 copy-done.7
  123.0 0.0 copy-done.9
  123.0 5.5 %finish_step.1 = (f32[3,1024]{1,0:T(4,128)}, f32[3,1024]{1,0:T(4,128)}, f32[3,1024]{1,0:T(4,128)}, f32[3,1024]{1,0:T(4,128)}) custom-call(s32[16,2,128]{2,1,0:T(2,128)S(1)} %get-tuple-element.8.counts.ids, f32[2,16,16,1,4,128]{5,4,3,2,1,0:T(4,128)S(1)} %deliver_forces.1.forces, f32[3,1024]{1,0:T(4,128)S(1)} %copy-done.1, f32[3,1024]{1,0:T(4,128)S(1)} %copy-done.3, ...), custom_call_target="tpu_custom_call" | custom-call | tf_op jit(solution)/shard_map/finish_step/pallas_call | solution.py:611
  (2 shorter events, 0.0 us)
Async XLA Ops:
  2.4 0.7 copy-start
  3.1 0.7 copy-start.2
  3.8 0.7 copy-start.4
  4.5 0.7 copy-start.6
  5.2 0.7 copy-start.8
  5.9 0.7 copy-start.10
  56.1 66.8 %copy-start.1 = (f32[3,1024]{1,0:T(4,128)S(1)}, f32[3,1024]{1,0:T(4,128)}, u32[]{:S(2)}) copy-start(f32[3,1024]{1,0:T(4,128)} %pos_in.3) | copy-start | bytes 36868
  56.1 66.8 %copy-start.3 = (f32[3,1024]{1,0:T(4,128)S(1)}, f32[3,1024]{1,0:T(4,128)}, u32[]{:S(2)}) copy-start(f32[3,1024]{1,0:T(4,128)} %vel_in.3) | copy-start | bytes 36868
  56.1 66.8 %copy-start.5 = (f32[3,1024]{1,0:T(4,128)S(1)}, f32[3,1024]{1,0:T(4,128)}, u32[]{:S(2)}) copy-start(f32[3,1024]{1,0:T(4,128)} %acc_in.3) | copy-start | bytes 36868
  56.2 66.8 %copy-start.7 = (f32[3,1024]{1,0:T(4,128)S(1)}, f32[3,1024]{1,0:T(4,128)}, u32[]{:S(2)}) copy-start(f32[3,1024]{1,0:T(4,128)} %jerk_in.3) | copy-start | bytes 36868
  56.2 66.8 %copy-start.9 = (f32[1,1024]{1,0:T(1,128)S(1)}, f32[1,1024]{1,0:T(1,128)}, u32[]{:S(2)}) copy-start(f32[1,1024]{1,0:T(1,128)} %step_in.3) | copy-start | bytes 12292

commit v4 on v3

--- a/solution.py
+++ b/solution.py
@@ -10,17 +10,13 @@
 TILE = 128
 EPS2 = 0.01
 LANES = 128
-BLOCK_J = 4096
-PIECE_J = 256
+BLOCK_J = 8192
+PIECE_J = 512
 PARTS = 16
 MESH = pl.DeviceIdType.MESH
 VMEM = pltpu.VMEM
 F32 = jnp.float32
 BF16 = jnp.bfloat16
-
-
-def anywhere():
-    return pl.BlockSpec(memory_space=pl.ANY)
 
 
 def vmem():
@@ -48,7 +44,7 @@
         self.col = lax.axis_index("col")
         self.spot, self.core = self.col // 2, lax.rem(self.col, 2)
         self.parity, self.layer = lax.rem(self.row, 2), self.row // 2
-        self.group = self.parity * self.plane + self.spot
+        self.group = self.spot * 2 + self.parity
         self.member = self.layer * 2 + self.core
         self.sibling = {"col": self.spot * 2 + 1 - self.core}
         self.twin = {"row": self.layer * 2 + 1 - self.parity}
@@ -94,32 +90,35 @@
     return norm, cross
 
 
-def group_sums(at, blocks, from_twin, from_spots, sends, recvs, meanwhile=None):
-    share = blocks.shape[0] // at.groups
-    span = share * at.plane
-    theirs = blocks.at[pl.ds((1 - at.parity) * span, span)]
-    remote(theirs, from_twin, sends.at[0], recvs.at[0], at.twin).start()
-    mine = pl.ds(at.parity * span, span)
-    await_bytes(from_twin, recvs.at[0])
-    blocks[mine] = blocks[mine] + from_twin[...]
-    from_spots[at.spot] = blocks[pl.ds(at.group * share, share)]
-
-    def to_spot(d):
+def greet(at):
+    z_at = lambda d: {"row": lax.rem(at.row + d + at.rows, at.rows)}
+    signal(at.sibling)
+    for d in (1, -1, 2, -2):
+        signal(z_at(d))
+    for d in range(1, at.plane):
+        signal(at.at_spot(lax.rem(at.spot + d, at.plane)))
+    count = 4 + at.plane
+
+    def tell(semaphore, far):
+        for d in (far, -far):
+            pl.semaphore_signal(semaphore, inc=1, device_id=z_at(d), device_id_type=MESH)
+
+    return count, tell
+
+
+def plane_sums(at, blocks, from_spots, send, recv, meanwhile):
+    span = blocks.shape[0] // at.plane
+    from_spots[at.spot] = blocks[pl.ds(at.spot * span, span)]
+    left = []
+    for d in range(1, at.plane):
         spot = lax.rem(at.spot + d, at.plane)
-        part = blocks.at[pl.ds(at.parity * span + spot * share, share)]
-        remote(part, from_spots.at[at.spot], sends.at[1], recvs.at[1], at.at_spot(spot)).start()
-
-    left = [(from_twin, sends.at[0])]
+        part = blocks.at[pl.ds(spot * span, span)]
+        remote(part, from_spots.at[at.spot], send, recv, at.at_spot(spot)).start()
+    meanwhile()
     if at.plane > 1:
-        for d in range(1, at.plane):
-            to_spot(d)
-        if meanwhile is not None:
-            meanwhile()
         rest = from_spots.at[pl.ds(0, at.plane - 1)]
-        await_bytes(rest, recvs.at[1])
-        left.append((rest, sends.at[1]))
-    elif meanwhile is not None:
-        meanwhile()
+        await_bytes(rest, recv)
+        left.append((rest, send))
     return jnp.sum(from_spots[...], axis=0), left
 
 
@@ -127,29 +126,22 @@
     rows,
     cols,
     total_stars,
-    pos_in,
-    vel_in,
-    acc_in,
-    jerk_in,
-    mass_in,
-    step_in,
-    msg,
+    x_pred,
+    v_pred,
+    mass,
+    lists,
+    live,
     ids,
     states,
     j_side,
     j_mass,
+    msg,
     shard,
     picked,
+    of_plane,
     from_twin,
     from_spots,
     table,
-    pos,
-    vel,
-    acc,
-    jerk,
-    mass,
-    step,
-    loads,
     sends,
     recvs,
     id_send,
@@ -157,31 +149,32 @@
     right_recv,
     left_recv,
     core_recv,
+    four,
+    eight,
 ):
     at = Place(rows, cols)
     me, mine, layers = at.member, at.group, at.layers
-    share = states.shape[0] // at.groups
-    pairs = ((pos_in, pos), (vel_in, vel), (acc_in, acc), (jerk_in, jerk), (mass_in, mass), (step_in, step))
-    loading = [pltpu.make_async_copy(source, target, loads.at[n]) for n, (source, target) in enumerate(pairs)]
-    for load in loading:
-        load.start()
-    signal(at.sibling)
-    for d in range(1, rows):
-        signal({"row": lax.rem(at.row + d, rows)})
-    for d in range(1, at.plane):
-        signal(at.at_spot(lax.rem(at.spot + d, at.plane)))
+    count, tell = greet(at)
+    tiles, unit = lists.shape[0], LANES // PARTS
+    at_tile = lax.broadcasted_iota(jnp.int32, lists.shape, 0)
+    diagonal = lax.broadcasted_iota(jnp.int32, lists.shape, 1) // unit == at_tile
+    named = jnp.where(at_tile < live[0], lists[...], -1)
+    parts = jnp.zeros_like(named)
+    for d in range(tiles):
+        turned = jnp.where(diagonal, pltpu.roll(named, unit * d, 1) if d else named, 0)
+        parts += pltpu.roll(turned, PARTS - d, 0) if d else turned
+    for p in range(PARTS):
+        msg[p, 0:1, :] = parts[p : p + 1, :]
+        msg[p, 1:2, :] = jnp.full((1, LANES), live[0], jnp.int32)
     ids[at.row] = msg[me]
-    for load in loading:
-        load.wait()
-    dt = step[...]
-    a, j, v = acc[...], jerk[...], vel[...]
-    shard[me, 0:3, :] = pos[...] + dt * (v + dt * (0.5 * a + dt * j / 6.0))
+    shard[me, 0:3, :] = x_pred[...]
     shard[me, 3:4, :] = mass[...] / total_stars
-    shard[me, 4:7, :] = v + dt * (a + dt * (0.5 * j))
-    shard[me, 7:8, :] = jnp.ones_like(dt)
-    await_greetings(rows + at.plane - 1)
-
-    width = pos.shape[1]
+    shard[me, 4:7, :] = v_pred[...]
+    shard[me, 7:8, :] = jnp.ones(mass.shape, F32)
+    await_greetings(count)
+    tell(four, 2)
+
+    width = mass.shape[1]
     chunks = width // LANES
 
     def prepare(z):
@@ -209,30 +202,40 @@
 
         each(0, 4 if both else 2, one)
 
-    def ring(s, way):
-        block = shard.at[lax.rem(at.layer - way * s + layers, layers) * 2 + at.core]
-        recv = (right_recv if way > 0 else left_recv).at[s]
+    def ring(s, way, part):
+        block = shard.at[lax.rem(at.layer - way * s + layers, layers) * 2 + at.core, :, part]
+        recv = (right_recv if way > 0 else left_recv).at[2 * s + (1 if part is halves[1] else 0)]
         return remote(block, block, sends.at[4], recv, at.in_layer(lax.rem(at.layer + way + layers, layers)))
 
-    def arrived(s, way):
-        block = shard.at[lax.rem(at.layer - way * (s + 1) + 2 * layers, layers) * 2 + at.core]
-        recv = (right_recv if way > 0 else left_recv).at[s]
+    def arrived(s, way, part):
+        block = shard.at[lax.rem(at.layer - way * (s + 1) + 2 * layers, layers) * 2 + at.core, :, part]
+        recv = (right_recv if way > 0 else left_recv).at[2 * s + (1 if part is halves[1] else 0)]
         remote(block, block, sends.at[4], recv, at.in_layer(lax.rem(at.layer + way + layers, layers))).wait_recv()
 
     def across(s, way, core):
         block = shard.at[lax.rem(at.layer - way * s + layers, layers) * 2 + core]
         return remote(block, block, sends.at[5], core_recv.at[2 * s + (1 - way) // 2], at.sibling)
 
+    halves = (pl.ds(0, width // 2), pl.ds(width // 2, width // 2))
     ways = (layers // 2, layers - 1 - layers // 2)
     for s in range(ways[0] + 1):
-        if s < ways[0]:
-            ring(s, 1).start()
-        if s < ways[1]:
-            ring(s, -1).start()
+        for part in halves:
+            if s:
+                arrived(s - 1, 1, part)
+            if 0 < s <= ways[1]:
+                arrived(s - 1, -1, part)
+            if s < ways[0]:
+                ring(s, 1, part).start()
+            if s < ways[1]:
+                ring(s, -1, part).start()
         across(s, 1, at.core).start()
         if 0 < s <= ways[1]:
             across(s, -1, at.core).start()
         if s == 0:
+            pl.semaphore_wait(four, 2)
+            tell(eight, 4)
+        elif s == 1:
+            pl.semaphore_wait(eight, 2)
 
             def send_ids(d):
                 peer = lax.rem(at.row + d, rows)
@@ -240,16 +243,12 @@
                 remote(part, ids.at[at.row], id_send, id_recv, {"row": peer}).start()
 
             each(1, rows, send_ids)
-        else:
+        if s:
             across(s - 1, 1, 1 - at.core).wait_recv()
             if 0 < s - 1 <= ways[1]:
                 across(s - 1, -1, 1 - at.core).wait_recv()
             if s < ways[0]:
                 prepare_layers(s - 1, 0 < s - 1 <= ways[1])
-        if s < ways[0]:
-            arrived(s, 1)
-        if s < ways[1]:
-            arrived(s, -1)
     across(ways[0], 1, 1 - at.core).wait_recv()
     id_rest = ids.at[pl.ds(0, rows - 1)]
     await_bytes(id_rest, id_recv)
@@ -268,7 +267,7 @@
         star = jnp.concatenate([ids[first + n, 0:1, :] for n in range(groups)], 1)
         owner = star // width
         row, col = owner // cols, lax.rem(owner, cols)
-        group = lax.rem(row, 2) * at.plane + col // 2
+        group = col // 2 * 2 + lax.rem(row, 2)
         member = row // 2 * 2 + lax.rem(col, 2)
         place = lax.rem(star, width)
         high = jnp.where((star >= 0) & (group == mine), place // LANES * PARTS + member, -1)
@@ -291,23 +290,23 @@
     def first_rest():
         prepare_layers(late, 0 < late <= ways[1])
 
-    total, left = group_sums(at, picked, from_twin, from_spots, sends, recvs, first_rest)
-    own = pl.ds(mine * share, share)
-    states[own] = total
-    span = at.plane * share
-    half = pl.ds(at.parity * span, span)
+    total, left = plane_sums(at, picked, from_spots, sends.at[0], recvs.at[0], first_rest)
+    span = total.shape[0]
+    own = pl.ds(at.spot * span, span)
+    of_plane[...] = total
+    remote(of_plane, from_twin, sends.at[1], recvs.at[1], at.twin).start()
+    await_bytes(from_twin, recvs.at[1])
+    states[own] = total + from_twin[...]
     for d in range(1, at.plane):
         spot = lax.rem(at.spot + d, at.plane)
         remote(states.at[own], states.at[own], sends.at[2], recvs.at[2], at.at_spot(spot)).start()
     prepare_layers(ways[0], False)
     if at.plane > 1:
-        rest = states.at[pl.ds(0, span - share)]
+        rest = states.at[pl.ds(0, states.shape[0] - span)]
         await_bytes(rest, recvs.at[2])
         left.append((rest, sends.at[2]))
-    remote(states.at[half], states.at[half], sends.at[3], recvs.at[3], at.twin).start()
-    await_bytes(states.at[half], recvs.at[3])
     left += [
-        (states.at[half], sends.at[3]),
+        (of_plane, sends.at[1]),
         (shard.at[pl.ds(0, layers - 1)], sends.at[4]),
         (shard.at[pl.ds(0, layers)], sends.at[5]),
         (id_rest, id_send),
@@ -405,19 +404,27 @@
     lax.fori_loop(0, (used + LANES - 1) // LANES, run, 0)
 
 
-def deliver_kernel(rows, cols, partial, out, blocks, from_twin, from_spots, lined, sends, recvs, plane_recv):
+def deliver_kernel(rows, cols, blocks, out, of_plane, from_twin, from_spots, lined, sends, recvs, plane_recv, four, eight):
     at = Place(rows, cols)
     plane = at.plane
-    signal(at.sibling)
-    for d in range(1, rows):
-        signal({"row": lax.rem(at.row + d, rows)})
-    for d in range(1, plane):
-        signal(at.at_spot(lax.rem(at.spot + d, plane)))
-    blocks[...] = partial[...]
-    await_greetings(rows + plane - 1)
-
-    total, left = group_sums(at, blocks, from_twin, from_spots, sends, recvs)
-    lined[at.row] = total
+    count, tell = greet(at)
+    await_greetings(count)
+    tell(four, 2)
+
+    def wider():
+        pl.semaphore_wait(four, 2)
+        tell(eight, 4)
+
+    total, left = plane_sums(at, blocks, from_spots, sends.at[0], recvs.at[0], wider)
+    share = total.shape[0] // 2
+    of_plane[...] = total
+    theirs = of_plane.at[pl.ds((1 - at.parity) * share, share)]
+    from_there = from_twin.at[pl.ds(0, share)]
+    remote(theirs, from_there, sends.at[5], recvs.at[5], at.twin).start()
+    left.append((theirs, sends.at[5]))
+    pl.semaphore_wait(eight, 2)
+    await_bytes(from_there, recvs.at[5])
+    lined[at.row] = of_plane[pl.ds(at.parity * share, share)] + from_there[...]
     mine = lined.at[at.row]
     for d in range(1, rows):
         remote(mine, mine, sends.at[2], recvs.at[2], {"row": lax.rem(at.row + d, rows)}).start()
@@ -445,39 +452,15 @@
 
 
 def finish_kernel(
-    rows,
-    cols,
-    counts,
-    forces,
-    pos_in,
-    vel_in,
-    acc_in,
-    jerk_in,
-    step_in,
-    new_pos,
-    new_vel,
-    new_acc,
-    new_jerk,
-    total,
-    lined,
-    pos,
-    vel,
-    acc,
-    jerk,
-    step,
-    loads,
+    rows, cols, counts, forces, pos, vel, acc, jerk, step, new_pos, new_vel, new_acc, new_jerk, total, lined
 ):
     at = Place(rows, cols)
-    pairs = ((pos_in, pos), (vel_in, vel), (acc_in, acc), (jerk_in, jerk), (step_in, step))
-    loading = [pltpu.make_async_copy(source, target, loads.at[n]) for n, (source, target) in enumerate(pairs)]
-    for load in loading:
-        load.start()
     width = pos.shape[1]
     highs = width // LANES
     mine = at.row * cols + at.col
     features = (0, 1, 2, 4, 5, 6)
     share = forces.shape[3]
-    together = 8
+    together = 16
     at8 = lax.broadcasted_iota(jnp.int32, (highs, LANES), 0)
     at_low = lax.broadcasted_iota(jnp.int32, (LANES, LANES), 0)
     total[...] = jnp.zeros_like(total)
@@ -490,8 +473,8 @@
             spots = []
             for b in range(2):
                 group = (2 * t + b) // share
-                z = member // 2 * 2 + group // at.plane
-                spots.append((lax.rem(member, 2), lax.rem(group, at.plane), z, lax.rem(2 * t + b, share)))
+                z = member // 2 * 2 + lax.rem(group, 2)
+                spots.append((lax.rem(member, 2), group // 2, z, lax.rem(2 * t + b, share)))
             star = forces[(*spots[0], slice(3, 4), slice(None))].astype(jnp.int32)
             ok = (star >= 0) & (star // width == mine)
             place = lax.rem(star, width)
@@ -523,8 +506,6 @@
         for c in range(highs):
             lined[order : order + 1, c * LANES : (c + 1) * LANES] = plane[c : c + 1, :]
 
-    for load in loading:
-        load.wait()
     on = lined[6:7, :] > 0.5
     a1, k1 = lined[0:3, :], lined[3:6, :]
     x, v, a, k, dt = pos[...], vel[...], acc[...], jerk[...], step[...]
@@ -546,26 +527,15 @@
     rows = lax.axis_size("row")
     cols = lax.axis_size("col")
     width = positions.shape[1]
-    tiles = active.shape[0] // TILE
-    unit = TILE // PARTS
     blocks = 2 * rows
     plane, layers = cols // 2, rows // 2
     share = blocks // (2 * plane)
     total_stars = width * rows * cols
-    dma = pltpu.SemaphoreType.DMA
-    triples = [VMEM((3, width), F32) for _ in range(4)]
-    single = VMEM((1, width), F32)
-    sum_scratch = [
-        VMEM((blocks, 4, LANES), F32),
-        VMEM((blocks // 2, 4, LANES), F32),
-        VMEM((plane, share, 4, LANES), F32),
-    ]
-
-    live = jnp.arange(tiles)[:, None] < live_tiles[0]
-    named = jnp.where(live, active.reshape(tiles, TILE), -1)
-    parts = named.reshape(tiles, PARTS, unit).transpose(1, 0, 2).reshape(PARTS, 1, LANES)
-    msg = jnp.concatenate([parts, jnp.broadcast_to(live_tiles[0], parts.shape)], 1)
-
+    dma, told = pltpu.SemaphoreType.DMA, pltpu.SemaphoreType.REGULAR
+    sum_scratch = [VMEM((2 * share, 4, LANES), F32)] * 2 + [VMEM((plane, 2 * share, 4, LANES), F32)]
+
+    x_pred = positions + elapsed * (velocities + elapsed * (0.5 * accels + elapsed * jerks / 6.0))
+    v_pred = velocities + elapsed * (accels + elapsed * jerks / 2.0)
     ids, states, j_side, j_mass = pl.pallas_call(
         functools.partial(gather_kernel, rows, cols, total_stars),
         out_shape=(
@@ -574,17 +544,17 @@
             jax.ShapeDtypeStruct((PARTS * width, LANES), BF16),
             jax.ShapeDtypeStruct((32, PARTS * width), BF16),
         ),
-        in_specs=[anywhere()] * 6 + [vmem()],
+        in_specs=[vmem()] * 4 + [smem()],
         out_specs=(vmem(),) * 4,
-        scratch_shapes=[VMEM((PARTS, 8, width), F32)]
+        scratch_shapes=[VMEM((PARTS, 2, LANES), jnp.int32), VMEM((PARTS, 8, width), F32), VMEM((blocks, 4, LANES), F32)]
         + sum_scratch
         + [VMEM((6 * PARTS * width // LANES, 3 * LANES), BF16)]
-        + triples
-        + [single, single, dma((6,)), dma((6,)), dma((4,)), dma, dma]
-        + [dma((layers,)), dma((layers,)), dma((2 * layers,))],
+        + [dma((6,)), dma((4,)), dma, dma]
+        + [dma((2 * layers,)) for _ in range(3)]
+        + [told, told],
         compiler_params=params(0),
         name="gather_states",
-    )(positions, velocities, accels, jerks, masses, elapsed, msg)
+    )(x_pred, v_pred, masses, active.reshape(active.shape[0] // TILE, TILE), live_tiles)
 
     pair_count = rows * LANES * PARTS * width
     partial = pl.pallas_call(
@@ -603,7 +573,7 @@
         out_shape=jax.ShapeDtypeStruct((2, plane, rows, share, 4, LANES), F32),
         in_specs=[vmem()],
         out_specs=vmem(),
-        scratch_shapes=sum_scratch + [VMEM((rows, share, 4, LANES), F32), dma((5,)), dma((5,)), dma((plane,))],
+        scratch_shapes=sum_scratch + [VMEM((rows, share, 4, LANES), F32), dma((6,)), dma((6,)), dma((plane,)), told, told],
         compiler_params=params(1),
         name="deliver_forces",
     )(partial)
@@ -611,9 +581,9 @@
     return pl.pallas_call(
         functools.partial(finish_kernel, rows, cols),
         out_shape=tuple(jax.ShapeDtypeStruct((3, width), F32) for _ in range(4)),
-        in_specs=[smem(), vmem()] + [anywhere()] * 5,
+        in_specs=[smem()] + [vmem()] * 6,
         out_specs=(vmem(),) * 4,
-        scratch_shapes=[VMEM((20 * width // LANES, LANES), F32), VMEM((8, width), F32)] + triples + [single, dma((5,))],
+        scratch_shapes=[VMEM((20 * width // LANES, LANES), F32), VMEM((8, width), F32)],
         compiler_params=params(),
         name="finish_step",
     )(ids, forces, positions, velocities, accels, jerks, elapsed)

time: 129 us -> 113 us (0.88)
  Pallas kernels: 122 us -> 109 us
  local copies, waits for them, and re-layouts: 5.24 us -> 1.41 us
    pallas_call x1, Pallas kernels: 49.5 us -> 44.6 us  [per_device(): pl.pallas_call(functools.partial(gather_kernel, rows, cols, total_stars),...]
    pallas_call x1, Pallas kernels: 31.4 us -> 27.9 us  [per_device(): pl.pallas_call(functools.partial(deliver_kernel, rows, cols), out_shape=j...]
    pallas_call x1, Pallas kernels: 35.4 us -> 32.3 us  [per_device(): pl.pallas_call(functools.partial(sweep_kernel, rows, cols), out_shape=jax...]
    unnamed x22 -> x14, local copies, waits for them, and re-layouts: 4.27 us -> 1.41 us
where the time goes in v4:
time: 113 us
  Pallas kernels  109 us (96%)
  local copies, waits for them, and re-layouts  1.41 us (1%)
  between operations  1.39 us (1%)
    pallas_call x1, Pallas kernels, per_device(): pl.pallas_call(functools.partial(gather_kernel, rows, cols, total_stars),...  44.6 us
    pallas_call x1, Pallas kernels, per_device(): pl.pallas_call(functools.partial(sweep_kernel, rows, cols), out_shape=jax...  32.3 us
    pallas_call x1, Pallas kernels, per_device(): pl.pallas_call(functools.partial(deliver_kernel, rows, cols), out_shape=j...  27.9 us
    pallas_call x1, Pallas kernels, per_device(): pl.pallas_call(functools.partial(finish_kernel, rows, cols), out_shape=tu...  4.31 us

profile of v4, /device:TPU:1, one launch (start us, length us, event | category | flops | bytes accessed | tf_op | source)
XLA Modules:
  0.0 112.7 jit_solution(8671686339972334766)
XLA Ops:
  1.3 0.8 multiply_add_fusion
  2.1 0.0 copy-start.5
  2.1 0.7 copy-done.5
  2.8 0.0 copy-start.6
  2.8 0.7 copy-done.6
  3.5 44.6 %gather_states.1 = (s32[16,2,128]{2,1,0:T(2,128)S(1)}, f32[32,4,128]{2,1,0:T(4,128)S(1)}, bf16[16384,128]{1,0:T(8,128)(2,1)S(1)}, bf16[32,16384]{1,0:T(8,128)(2,1)S(1)}) custom-call(f32[3,1024]{1,0:T(4,128)S(1)} %get-tuple-element.13.x_pred, f32[3,1024]{1,0:T(4,128)S(1)} %get-tuple-element.12.v_pred, f32[1,1024]{1,0:T(1,128)S(1)} %copy-done.6, ...), custom_call_target="tpu_custom_call" | custom-call | tf_op jit(solution)/shard_map/gather_states/pallas_call | solution.py:539
  48.1 0.0 copy-start
  48.1 0.0 copy-start.1
  48.2 0.0 copy-start.2
  48.2 0.0 copy-start.3
  48.2 0.0 copy-start.4
  48.2 32.3 %pair_sums.1.blocks = f32[32,4,128]{2,1,0:T(4,128)S(1)} custom-call(s32[16,2,128]{2,1,0:T(2,128)S(1)} %get-tuple-element.8.counts.ids, s32[16,2,128]{2,1,0:T(2,128)S(1)} %get-tuple-element.8.counts.ids, f32[32,4,128]{2,1,0:T(4,128)S(1)} %get-tuple-element.9.states, bf16[16384,128]{1,0:T(8,128)(2,1)S(1)} %get-tuple-element.10.j_side, ...), custom_call_target="tpu_custom_call" | custom-call | flops 6710886400 | bytes 1048576 | tf_op jit(solution)/shard_map/pair_sums/pallas_call | solution.py:560
  80.5 27.9 %deliver_forces.1.forces = f32[2,16,16,1,4,128]{5,4,3,2,1,0:T(4,128)S(1)} custom-call(f32[32,4,128]{2,1,0:T(4,128)S(1)} %pair_sums.1.blocks), custom_call_target="tpu_custom_call" | custom-call | tf_op jit(solution)/shard_map/deliver_forces/pallas_call | solution.py:571
  108.4 0.0 copy-done
  108.4 0.0 copy-done.1
  108.4 0.0 copy-done.2
  108.4 0.0 copy-done.3
  108.4 0.0 copy-done.4
  108.4 4.3 %finish_step.1 = (f32[3,1024]{1,0:T(4,128)}, f32[3,1024]{1,0:T(4,128)}, f32[3,1024]{1,0:T(4,128)}, f32[3,1024]{1,0:T(4,128)}) custom-call(s32[16,2,128]{2,1,0:T(2,128)S(1)} %get-tuple-element.8.counts.ids, f32[2,16,16,1,4,128]{5,4,3,2,1,0:T(4,128)S(1)} %deliver_forces.1.forces, f32[3,1024]{1,0:T(4,128)S(1)} %copy-done.3, f32[3,1024]{1,0:T(4,128)S(1)} %copy-done, ...), custom_call_target="tpu_custom_call" | custom-call | tf_op jit(solution)/shard_map/finish_step/pallas_call | solution.py:581
Async XLA Ops:
  2.1 0.7 copy-start.5
  2.8 0.7 copy-start.6
  48.1 60.2 %copy-start = (f32[3,1024]{1,0:T(4,128)S(1)}, f32[3,1024]{1,0:T(4,128)}, u32[]{:S(2)}) copy-start(f32[3,1024]{1,0:T(4,128)} %vel.1) | copy-start | bytes 36868
  48.1 60.2 %copy-start.1 = (f32[3,1024]{1,0:T(4,128)S(1)}, f32[3,1024]{1,0:T(4,128)}, u32[]{:S(2)}) copy-start(f32[3,1024]{1,0:T(4,128)} %acc.1) | copy-start | bytes 36868
  48.2 60.2 %copy-start.2 = (f32[3,1024]{1,0:T(4,128)S(1)}, f32[3,1024]{1,0:T(4,128)}, u32[]{:S(2)}) copy-start(f32[3,1024]{1,0:T(4,128)} %jerk.1) | copy-start | bytes 36868
  48.2 60.2 %copy-start.3 = (f32[3,1024]{1,0:T(4,128)S(1)}, f32[3,1024]{1,0:T(4,128)}, u32[]{:S(2)}) copy-start(f32[3,1024]{1,0:T(4,128)} %pos.1) | copy-start | bytes 36868
  48.2 60.2 %copy-start.4 = (f32[1,1024]{1,0:T(1,128)S(1)}, f32[1,1024]{1,0:T(1,128)}, u32[]{:S(2)}) copy-start(f32[1,1024]{1,0:T(1,128)} %step.1) | copy-start | bytes 12292

commit v5 on v4

--- a/solution.py
+++ b/solution.py
@@ -10,7 +10,7 @@
 TILE = 128
 EPS2 = 0.01
 LANES = 128
-BLOCK_J = 8192
+BLOCK_J = 16384
 PIECE_J = 512
 PARTS = 16
 MESH = pl.DeviceIdType.MESH
@@ -255,7 +255,7 @@
 
     high_count = PARTS * chunks
     features = (0, 1, 2, 4, 5, 6)
-    groups = min(4, rows)
+    groups = min(8, rows)
     for order, f in enumerate(features):
         plane = jnp.concatenate([shard[:, f, c * LANES : (c + 1) * LANES] for c in range(chunks)], 0)
         h, m, l = split3(plane)

time: 113 us -> 106 us (0.938)
  Pallas kernels: 109 us -> 102 us
    pallas_call x1, Pallas kernels: 32.3 us -> 26.4 us  [per_device(): pl.pallas_call(functools.partial(sweep_kernel, rows, cols), out_shape=jax...]
where the time goes in v5:
time: 106 us
  Pallas kernels  102 us (96%)
  local copies, waits for them, and re-layouts  1.41 us (1%)
  between operations  1.39 us (1%)
    pallas_call x1, Pallas kernels, per_device(): pl.pallas_call(functools.partial(gather_kernel, rows, cols, total_stars),...  44.3 us
    pallas_call x1, Pallas kernels, per_device(): pl.pallas_call(functools.partial(deliver_kernel, rows, cols), out_shape=j...  27.9 us
    pallas_call x1, Pallas kernels, per_device(): pl.pallas_call(functools.partial(sweep_kernel, rows, cols), out_shape=jax...  26.4 us
    pallas_call x1, Pallas kernels, per_device(): pl.pallas_call(functools.partial(finish_kernel, rows, cols), out_shape=tu...  3.85 us

profile of v5, /device:TPU:1, one launch (start us, length us, event | category | flops | bytes accessed | tf_op | source)
XLA Modules:
  0.0 106.1 jit_solution(11238210865062703899)
XLA Ops:
  1.3 0.8 multiply_add_fusion
  2.1 0.0 copy-start.5
  2.1 0.7 copy-done.5
  2.8 0.0 copy-start.6
  2.8 0.7 copy-done.6
  3.5 44.3 %gather_states.1 = (s32[16,2,128]{2,1,0:T(2,128)S(1)}, f32[32,4,128]{2,1,0:T(4,128)S(1)}, bf16[16384,128]{1,0:T(8,128)(2,1)S(1)}, bf16[32,16384]{1,0:T(8,128)(2,1)S(1)}) custom-call(f32[3,1024]{1,0:T(4,128)S(1)} %get-tuple-element.13.x_pred, f32[3,1024]{1,0:T(4,128)S(1)} %get-tuple-element.12.v_pred, f32[1,1024]{1,0:T(1,128)S(1)} %copy-done.6, ...), custom_call_target="tpu_custom_call" | custom-call | tf_op jit(solution)/shard_map/gather_states/pallas_call | solution.py:539
  47.8 0.0 copy-start
  47.8 0.0 copy-start.1
  47.9 0.0 copy-start.2
  47.9 0.0 copy-start.3
  47.9 0.0 copy-start.4
  47.9 26.4 %pair_sums.1.blocks = f32[32,4,128]{2,1,0:T(4,128)S(1)} custom-call(s32[16,2,128]{2,1,0:T(2,128)S(1)} %get-tuple-element.8.counts.ids, s32[16,2,128]{2,1,0:T(2,128)S(1)} %get-tuple-element.8.counts.ids, f32[32,4,128]{2,1,0:T(4,128)S(1)} %get-tuple-element.9.states, bf16[16384,128]{1,0:T(8,128)(2,1)S(1)} %get-tuple-element.10.j_side, ...), custom_call_target="tpu_custom_call" | custom-call | flops 6710886400 | bytes 1048576 | tf_op jit(solution)/shard_map/pair_sums/pallas_call | solution.py:560
  74.3 27.9 %deliver_forces.1.forces = f32[2,16,16,1,4,128]{5,4,3,2,1,0:T(4,128)S(1)} custom-call(f32[32,4,128]{2,1,0:T(4,128)S(1)} %pair_sums.1.blocks), custom_call_target="tpu_custom_call" | custom-call | tf_op jit(solution)/shard_map/deliver_forces/pallas_call | solution.py:571
  102.2 0.0 copy-done
  102.2 0.0 copy-done.1
  102.2 0.0 copy-done.2
  102.2 0.0 copy-done.3
  102.2 0.0 copy-done.4
  102.2 3.9 %finish_step.1 = (f32[3,1024]{1,0:T(4,128)}, f32[3,1024]{1,0:T(4,128)}, f32[3,1024]{1,0:T(4,128)}, f32[3,1024]{1,0:T(4,128)}) custom-call(s32[16,2,128]{2,1,0:T(2,128)S(1)} %get-tuple-element.8.counts.ids, f32[2,16,16,1,4,128]{5,4,3,2,1,0:T(4,128)S(1)} %deliver_forces.1.forces, f32[3,1024]{1,0:T(4,128)S(1)} %copy-done.3, f32[3,1024]{1,0:T(4,128)S(1)} %copy-done, ...), custom_call_target="tpu_custom_call" | custom-call | tf_op jit(solution)/shard_map/finish_step/pallas_call | solution.py:581
Async XLA Ops:
  2.1 0.7 copy-start.5
  2.8 0.7 copy-start.6
  47.8 54.3 %copy-start = (f32[3,1024]{1,0:T(4,128)S(1)}, f32[3,1024]{1,0:T(4,128)}, u32[]{:S(2)}) copy-start(f32[3,1024]{1,0:T(4,128)} %vel.1) | copy-start | bytes 36868
  47.8 54.3 %copy-start.1 = (f32[3,1024]{1,0:T(4,128)S(1)}, f32[3,1024]{1,0:T(4,128)}, u32[]{:S(2)}) copy-start(f32[3,1024]{1,0:T(4,128)} %acc.1) | copy-start | bytes 36868
  47.9 54.3 %copy-start.2 = (f32[3,1024]{1,0:T(4,128)S(1)}, f32[3,1024]{1,0:T(4,128)}, u32[]{:S(2)}) copy-start(f32[3,1024]{1,0:T(4,128)} %jerk.1) | copy-start | bytes 36868
  47.9 54.3 %copy-start.3 = (f32[3,1024]{1,0:T(4,128)S(1)}, f32[3,1024]{1,0:T(4,128)}, u32[]{:S(2)}) copy-start(f32[3,1024]{1,0:T(4,128)} %pos.1) | copy-start | bytes 36868
  47.9 54.3 %copy-start.4 = (f32[1,1024]{1,0:T(1,128)S(1)}, f32[1,1024]{1,0:T(1,128)}, u32[]{:S(2)}) copy-start(f32[1,1024]{1,0:T(1,128)} %step.1) | copy-start | bytes 12292
